TPU v7x, 32 devices: a whole 2x2x4 slice. The times are simulated.
32 devices in a mesh: section: 2 (over y), segment: 4 (over x, core), fsdp: 4 (over z).
Axes of the slice: x: 2, y: 2, z: 4, core: 2. Of those that a mesh axis runs over, the one named last changes fastest.
Arguments:
- out_grad: bfloat16 [2, 4, 256, 6144], P(None, 'fsdp'), may hold values from -48 to 48
- queries: bfloat16 [2, 4, 256, 6144], P(None, 'fsdp', None, 'segment'), may hold values from -40 to 40
- enc_keys: bfloat16 [2, 4, 256, 6144], P(None, 'fsdp', None, 'segment'), may hold values from -4 to 4
- enc_values: bfloat16 [2, 4, 256, 6144], P(None, 'fsdp', None, 'segment'), may hold values from -6 to 6
- key_mask: int32 [2, 4, 256], P(None, 'fsdp'), may hold values from 0 to 1, as said below
- weights: bfloat16 [2, 2, 6144, 6144], P('section', None, 'fsdp', 'segment'), may hold values from -0.078125 to 0.078125
Outputs:
- grads: bfloat16 [2, 2, 4, 256, 6144], P('section', None, 'fsdp', None, 'segment')
Inputs may be any that keep to these rules, and one draw needn't show every extreme that they name: `key_mask`: each row is 1 on a prefix of 128 or more positions and 0 after it; the first reaction of every microbatch has no padding.
All inputs are finite; a program needn't handle non-finite values.
Results may differ from a plain program's by a relative error of at most 0.014.
Values may be sent and summed in bfloat16 or wider, within the bound.
A program may use at most 192 MiB of HBM per device.

v0:
```python
import jax
import jax.numpy as jnp
from jax import lax
from jax.sharding import PartitionSpec as P

HDIM = 128


def passed_along(value, axis, by):
    peers = lax.axis_size(axis)
    pairs = [(i, i + by) for i in range(peers) if 0 <= i + by < peers]
    return lax.ppermute(value, axis, pairs)


def attend(grad_rows, first_weight, queries, enc_keys, enc_values, key_mask):
    reaction_count, seq_length, local_width = queries.shape
    head_count = local_width // HDIM
    score_scale = HDIM ** (-0.5)
    ctx_grad = jnp.dot(grad_rows, first_weight, preferred_element_type=jnp.float32).astype(
        jnp.bfloat16
    )
    shaped = (reaction_count, seq_length, head_count, HDIM)
    grad_heads = ctx_grad.reshape(shaped)
    query_heads = queries.reshape(shaped)
    key_heads = enc_keys.reshape(shaped)
    value_heads = enc_values.reshape(shaped)
    scores = (
        jnp.einsum("bihc,bjhc->bhij", query_heads, key_heads, preferred_element_type=jnp.float32)
        * score_scale
    )
    scores = jnp.where(key_mask[:, None, None, :] > 0, scores, -jnp.inf)
    row_top = jnp.max(scores, axis=-1, keepdims=True)
    exp_scores = jnp.exp(scores - row_top)
    probabilities = exp_scores / jnp.sum(exp_scores, axis=-1, keepdims=True)
    probs_half = probabilities.astype(jnp.bfloat16)
    prob_grad = jnp.einsum(
        "bihc,bjhc->bhij", grad_heads, value_heads, preferred_element_type=jnp.float32
    )
    center = jnp.sum(probabilities * prob_grad, axis=-1, keepdims=True)
    score_grad = (probabilities * (prob_grad - center)).astype(jnp.bfloat16)
    query_grad = (
        jnp.einsum("bhij,bjhc->bihc", score_grad, key_heads, preferred_element_type=jnp.float32)
        * score_scale
    ).astype(jnp.bfloat16)
    key_grad = (
        jnp.einsum("bhij,bihc->bjhc", score_grad, query_heads, preferred_element_type=jnp.float32)
        * score_scale
    ).astype(jnp.bfloat16)
    value_grad = jnp.einsum(
        "bhij,bihc->bjhc", probs_half, grad_heads, preferred_element_type=jnp.float32
    ).astype(jnp.bfloat16)
    flat = (reaction_count * seq_length, local_width)
    return (query_grad.reshape(flat), key_grad.reshape(flat), value_grad.reshape(flat))


def project(grad_rows, weight_cols):
    return lax.dot_general(
        grad_rows, weight_cols, (((1,), (1,)), ((), ())), preferred_element_type=jnp.float32
    )


def per_device(out_grad, queries, enc_keys, enc_values, key_mask, weights):
    decoder = lax.axis_index("section") == 1
    gathered = lax.all_gather(weights, "fsdp", axis=2, tiled=True)
    first_weight = gathered[0, 0]
    second_weight = gathered[0, 1]
    micro_count, reaction_count, seq_length, feature_width = out_grad.shape
    local_width = queries.shape[3]
    row_count = reaction_count * seq_length
    blank_grads = jnp.zeros((row_count, local_width), jnp.bfloat16)
    held_grads = (blank_grads, blank_grads)
    sums_list = []
    for tick_index in range(micro_count + 1):
        has_decoder = tick_index < micro_count
        has_encoder = tick_index > 0

        def decoder_tick(tick_index=tick_index):
            query_grad, key_grad, value_grad = attend(
                out_grad[tick_index].reshape(row_count, feature_width),
                first_weight,
                queries[tick_index],
                enc_keys[tick_index],
                enc_values[tick_index],
                key_mask[tick_index],
            )
            return (key_grad, value_grad, project(query_grad, second_weight))

        def encoder_tick(held_grads=held_grads):
            return (
                blank_grads,
                blank_grads,
                project(held_grads[0], first_weight) + project(held_grads[1], second_weight),
            )

        def empty_tick():
            return (blank_grads, blank_grads, jnp.zeros((row_count, feature_width), jnp.float32))

        if has_decoder and has_encoder:
            key_grad, value_grad, partial_sum = lax.cond(decoder, decoder_tick, encoder_tick)
        elif has_decoder:
            key_grad, value_grad, partial_sum = lax.cond(decoder, decoder_tick, empty_tick)
        else:
            key_grad, value_grad, partial_sum = lax.cond(decoder, empty_tick, encoder_tick)
        summed = lax.psum_scatter(
            partial_sum.astype(jnp.bfloat16), "segment", scatter_dimension=1, tiled=True
        ).astype(jnp.float32)
        sums_list.append(summed)
        if has_decoder:
            held_grads = passed_along((key_grad, value_grad), "section", -1)
    decoder_stack = jnp.stack(sums_list[:micro_count])
    encoder_stack = jnp.stack(sums_list[1:])
    chosen = jnp.where(decoder, decoder_stack, encoder_stack).astype(jnp.bfloat16)
    result = chosen.reshape(1, micro_count, reaction_count, seq_length, chosen.shape[2])
    return result


def solution(mesh):
    return jax.shard_map(
        per_device,
        mesh=mesh,
        in_specs=(
            P(None, "fsdp", None, None),
            P(None, "fsdp", None, "segment"),
            P(None, "fsdp", None, "segment"),
            P(None, "fsdp", None, "segment"),
            P(None, "fsdp", None),
            P("section", None, "fsdp", "segment"),
        ),
        out_specs=P("section", None, "fsdp", None, "segment"),
        check_vma=False,
    )
```

profile of v0, /device:TPU:0, one launch (start us, length us, event | category | flops | bytes accessed | tf_op | source)
XLA Modules:
  0.0 885.6 jit_solution(10194121533391093433)
XLA Ops:
  7.9 1.6 copy.41
  9.5 1.6 copy.42
  11.1 1.6 copy.43
  12.7 630.9 %all-gather.2.cloned.1.call-done = bf16[1,2,6144,1536]{3,2,1,0:T(8,128)(2,1)} async-done(((bf16[1,2,1536,1536]{3,2,1,0:T(8,128)(2,1)}), bf16[1,2,6144,1536]{3,2,1,0:T(8,128)(2,1)}) %all-gather.2.cloned.1.call-update) | async-done | bytes 37748752 | tf_op jit(solution)/shard_map/all_gather | solution.py:64
  643.5 26.3 %slice_bitcast_fusion = (bf16[6144,1536]{1,0:T(8,128)(2,1)}, bf16[6144,1536]{1,0:T(8,128)(2,1)}) fusion(bf16[1,2,6144,1536]{3,2,1,0:T(8,128)(2,1)} %all-gather.2.cloned.1.call-done), kind=kLoop, calls=%fused_computation.48 | loop fusion | bytes 75497472 | tf_op jit(solution)/shard_map/squeeze | solution.py:66
  669.8 2.3 conditional.3
  672.1 1.7 copy-done
  673.9 2.5 copy.44
  677.6 2.3 copy.45
  681.2 48.4 %collective-permute-done = bf16[256,1536]{1,0:T(8,128)(2,1)} collective-permute-done((bf16[256,1536]{1,0:T(8,128)(2,1)}, bf16[256,1536]{1,0:T(8,128)(2,1)}, u32[]{:S(2)}, u32[]{:S(2)}) %collective-permute-start) | collective-permute-done | bytes 786464 | tf_op jit(solution)/shard_map/ppermute | solution.py:12
  729.6 15.9 %collective-permute-done.1 = bf16[256,1536]{1,0:T(8,128)(2,1)S(1)} collective-permute-done((bf16[256,1536]{1,0:T(8,128)(2,1)}, bf16[256,1536]{1,0:T(8,128)(2,1)S(1)}, u32[]{:S(2)}, u32[]{:S(2)}) %collective-permute-start.1) | collective-permute-done | bytes 786464 | tf_op jit(solution)/shard_map/ppermute | solution.py:12
  745.6 24.9 %conditional.4 = (bf16[256,1536]{0,1:T(8,128)(2,1)}, bf16[256,1536]{0,1:T(8,128)(2,1)}, bf16[256,6144]{1,0:T(8,128)(2,1)}) conditional(s32[]{:T(128)} %convert_element_type.115, (bf16[256,1536]{1,0:T(8,128)(2,1)}, bf16[6144,1536]{1,0:T(8,128)(2,1)}, bf16[256,1536]{1,0:T(8,128)(2,1)S(1)}, bf16[6144,1536]{1,0:T(8,128)(2,1)}) %tuple.29, ...), branch_computations={%region_6.7_spmd, %region_7.11_spmd} | conditional | flops 10682890240 | bytes 111748784 | solution.py:99
  745.6 10.9 %fusion.43 = f32[256,6144]{1,0:T(8,128)} fusion(bf16[256,1536]{1,0:T(8,128)(2,1)} %get-tuple-element.59, bf16[6144,1536]{1,0:T(8,128)(2,1)} %get-tuple-element.60), kind=kOutput, calls=%fused_computation.57 | convolution fusion | flops 4831838208 | bytes 25952256 | tf_op jit(solution)/shard_map/cond/branch_0_fun/dot_general | solution.py:57
  756.5 12.0 %convolution_add_fusion = bf16[256,6144]{1,0:T(8,128)(2,1)} fusion(f32[256,6144]{1,0:T(8,128)} %fusion.43, bf16[256,1536]{1,0:T(8,128)(2,1)S(1)} %get-tuple-element.61, bf16[6144,1536]{1,0:T(8,128)(2,1)} %get-tuple-element.62), kind=kOutput, calls=%fused_computation | convolution fusion | flops 4834983936 | bytes 29097984 | tf_op jit(solution)/shard_map/cond/branch_0_fun/dot_general | solution.py:57
  770.5 1.4 copy.49
  773.2 1.4 copy.50
  775.9 23.8 %collective-permute-done.2 = bf16[256,1536]{1,0:T(8,128)(2,1)S(1)} collective-permute-done((bf16[256,1536]{1,0:T(8,128)(2,1)S(1)}, bf16[256,1536]{1,0:T(8,128)(2,1)S(1)}, u32[]{:S(2)}, u32[]{:S(2)}) %collective-permute-start.2) | collective-permute-done | bytes 786464 | tf_op jit(solution)/shard_map/ppermute | solution.py:12
  799.8 15.4 %collective-permute-done.3 = bf16[256,1536]{1,0:T(8,128)(2,1)S(1)} collective-permute-done((bf16[256,1536]{1,0:T(8,128)(2,1)S(1)}, bf16[256,1536]{1,0:T(8,128)(2,1)S(1)}, u32[]{:S(2)}, u32[]{:S(2)}) %collective-permute-start.3) | collective-permute-done | bytes 786464 | tf_op jit(solution)/shard_map/ppermute | solution.py:12
  815.2 22.6 %conditional.5 = (bf16[256,6144]{1,0:T(8,128)(2,1)S(1)}) conditional(s32[]{:T(128)} %convert_element_type.115, (bf16[256,1536]{1,0:T(8,128)(2,1)S(1)}, bf16[6144,1536]{1,0:T(8,128)(2,1)}, bf16[256,1536]{1,0:T(8,128)(2,1)S(1)}, bf16[6144,1536]{1,0:T(8,128)(2,1)}) %tuple.30, () %tuple.31), branch_computations={%region_12.13_spmd, %region_13.14_spmd} | conditional | flops 9666822144 | bytes 55050248 | solution.py:103
  815.2 11.7 %fusion.44 = f32[256,6144]{1,0:T(8,128)} fusion(bf16[256,1536]{1,0:T(8,128)(2,1)S(1)} %get-tuple-element.70, bf16[6144,1536]{1,0:T(8,128)(2,1)} %get-tuple-element.71), kind=kOutput, calls=%fused_computation.58 | convolution fusion | flops 4831838208 | bytes 25952256 | tf_op jit(solution)/shard_map/cond/branch_0_fun/dot_general | solution.py:57
  826.9 10.9 %convolution_add_fusion.1 = bf16[256,6144]{1,0:T(8,128)(2,1)S(1)} fusion(f32[256,6144]{1,0:T(8,128)} %fusion.44, bf16[256,1536]{1,0:T(8,128)(2,1)S(1)} %get-tuple-element.72, bf16[6144,1536]{1,0:T(8,128)(2,1)} %get-tuple-element.73), kind=kOutput, calls=%fused_computation.1 | convolution fusion | flops 4834983936 | bytes 29097984 | tf_op jit(solution)/shard_map/cond/branch_0_fun/dot_general | solution.py:57
  837.8 1.6 copy-done.5
  839.5 36.3 %reduce-scatter.8.cloned.1.call-done = bf16[256,1536]{1,0:T(8,128)(2,1)} async-done(((bf16[256,6144]{1,0:T(8,128)(2,1)}), bf16[256,1536]{1,0:T(8,128)(2,1)}) %reduce-scatter.8.cloned.1.call-update) | async-done | bytes 786448 | tf_op jit(solution)/shard_map/reduce_scatter | solution.py:104
  875.8 3.3 fusion.40
  (33 shorter events, 10.9 us)
Async XLA Ops:
  6.5 1.4 copy-start.13
  6.5 637.0 %all-gather.2.cloned.1.call-start = ((), (), s32[]{:S(2)}) async-start(), calls=%async_computation.3 | async-start | bytes 47185920 | tf_op jit(solution)/shard_map/all_gather | solution.py:64
  7.3 2.2 copy-start.14
  7.3 832.2 %reduce-scatter.4.cloned.1.call-start = ((), (), s32[]{:S(2)}) async-start(), calls=%async_computation.4 | async-start | bytes 3932160 | tf_op jit(solution)/shard_map/reduce_scatter | solution.py:104
  9.5 1.6 copy-start.15
  12.6 657.2 %copy-start.18 = (s32[2,1,256]{2,1,0:T(1,128)S(1)}, s32[2,1,256]{2,1,0:T(1,128)}, u32[]{:S(2)}) copy-start(s32[2,1,256]{2,1,0:T(1,128)} %param.16) | copy-start | bytes 6148
  672.1 1.7 copy-start
  673.8 71.7 %copy-start.1 = (bf16[2,1,256,1536]{2,3,1,0:T(8,128)(2,1)S(1)}, bf16[2,1,256,1536]{2,3,1,0:T(8,128)(2,1)}, u32[]{:S(2)}) copy-start(bf16[2,1,256,1536]{2,3,1,0:T(8,128)(2,1)} %copy.41) | copy-start | bytes 4718596
  673.8 71.7 %copy-start.2 = (bf16[2,1,256,1536]{2,3,1,0:T(8,128)(2,1)S(1)}, bf16[2,1,256,1536]{2,3,1,0:T(8,128)(2,1)}, u32[]{:S(2)}) copy-start(bf16[2,1,256,1536]{2,3,1,0:T(8,128)(2,1)} %copy.42) | copy-start | bytes 4718596
  673.8 165.7 %reduce-scatter.6.cloned.1.call-start = ((), (), s32[]{:S(2)}) async-start(), calls=%async_computation.5 | async-start | bytes 3932160 | tf_op jit(solution)/shard_map/reduce_scatter | solution.py:104
  676.4 53.3 %collective-permute-start = (bf16[256,1536]{1,0:T(8,128)(2,1)}, bf16[256,1536]{1,0:T(8,128)(2,1)}, u32[]{:S(2)}, u32[]{:S(2)}) collective-permute-start(bf16[256,1536]{1,0:T(8,128)(2,1)} %copy.44), channel_id=1, source_target_pairs={{16,0},{17,1},{18,2},{19,3},{20,4},{21,5},{22,6},{23,7},{24,8},{25... | collective-permute-start | bytes 2359304 | tf_op jit(solution)/shard_map/ppermute | solution.py:12
  679.9 65.6 %collective-permute-start.1 = (bf16[256,1536]{1,0:T(8,128)(2,1)}, bf16[256,1536]{1,0:T(8,128)(2,1)S(1)}, u32[]{:S(2)}, u32[]{:S(2)}) collective-permute-start(bf16[256,1536]{1,0:T(8,128)(2,1)} %copy.45), channel_id=1, source_target_pairs={{16,0},{17,1},{18,2},{19,3},{20,4},{21,5},{22,6},{23,7},{24,8},{25... | collective-permute-start | bytes 2359304 | tf_op jit(solution)/shard_map/ppermute | solution.py:12
  770.5 105.4 %reduce-scatter.8.cloned.1.call-start = ((), (), s32[]{:S(2)}) async-start(), calls=%async_computation.6 | async-start | bytes 3932160 | tf_op jit(solution)/shard_map/reduce_scatter | solution.py:104
  771.9 27.9 %collective-permute-start.2 = (bf16[256,1536]{1,0:T(8,128)(2,1)S(1)}, bf16[256,1536]{1,0:T(8,128)(2,1)S(1)}, u32[]{:S(2)}, u32[]{:S(2)}) collective-permute-start(bf16[256,1536]{1,0:T(8,128)(2,1)S(1)} %copy.49), channel_id=1, source_target_pairs={{16,0},{17,1},{18,2},{19,3},{20,4},{21,5},{22,6},{23,7},{24,8},{25... | collective-permute-start | bytes 2359304 | tf_op jit(solution)/shard_map/ppermute | solution.py:12
  774.6 40.5 %collective-permute-start.3 = (bf16[256,1536]{1,0:T(8,128)(2,1)S(1)}, bf16[256,1536]{1,0:T(8,128)(2,1)S(1)}, u32[]{:S(2)}, u32[]{:S(2)}) collective-permute-start(bf16[256,1536]{1,0:T(8,128)(2,1)S(1)} %copy.50), channel_id=1, source_target_pairs={{16,0},{17,1},{18,2},{19,3},{20,4},{21,5},{22,6},{23,7},{24,8},{25... | collective-permute-start | bytes 2359304 | tf_op jit(solution)/shard_map/ppermute | solution.py:12
  837.8 1.6 copy-start.5
Sparse Core Ops, SparseCore 0:
  8.9 634.5 all-gather.1
  673.9 68.6 reduce-scatter.3
  770.6 43.5 reduce-scatter.5
  839.6 36.2 reduce-scatter.7
where the time goes:
time: 886 us
  waiting for transfers between devices  772 us (87%)
  local copies, waits for them, and re-layouts  46.7 us (5%)
  matrix products  45.6 us (5%)
  between operations  13.2 us (1%)
    all_gather x1, waiting for transfers between devices, per_device(): gathered = lax.all_gather(weights, 'fsdp', axis=2, tiled=True)  631 us
    ppermute x4, waiting for transfers between devices, passed_along(): return lax.ppermute(value, axis, pairs)  104 us
    dot_general x4, matrix products, project(): lax.dot_general(grad_rows, weight_cols, (((1,), (1,)), ((), ())), preferr...  45.6 us
    reduce_scatter x3, waiting for transfers between devices, per_device(): lax.psum_scatter(partial_sum.astype(jnp.bfloat16), 'segment', scatter_dim...  36.4 us
    squeeze x1, local copies, waits for them, and re-layouts, per_device(): second_weight = gathered[0, 1]  26.3 us
  transfers between devices with their start and end apart: 8, of which 6 were waited for; matrix products, arithmetic and copies ran while one was open for 7% of the time, Pallas kernels for 0%

commit v1 on v0

v1 whole, which is shorter than its diff:
```python
import functools

import jax
import jax.numpy as jnp
from jax import lax
from jax.experimental import pallas as pl
from jax.experimental.pallas import tpu as pltpu
from jax.sharding import PartitionSpec as P

HDIM = 128


def head_grads(mask_ref, grad_ref, query_ref, key_ref, value_ref, dq_ref, dk_ref, dv_ref):
    scale = HDIM ** (-0.5)
    f32 = jnp.float32

    def rows_rows(a, b):
        return lax.dot_general(a, b, (((1,), (1,)), ((), ())), preferred_element_type=f32)

    def cols_rows(a, b):
        return lax.dot_general(a, b, (((0,), (0,)), ((), ())), preferred_element_type=f32)

    grad, query, key, value = grad_ref[...], query_ref[...], key_ref[...], value_ref[...]
    scores = rows_rows(query, key) * scale
    scores = jnp.where(mask_ref[...] > 0, scores, -jnp.inf)
    exp_scores = jnp.exp(scores - jnp.max(scores, axis=-1, keepdims=True))
    probs = exp_scores / jnp.sum(exp_scores, axis=-1, keepdims=True)
    prob_grad = rows_rows(grad, value)
    center = jnp.sum(probs * prob_grad, axis=-1, keepdims=True)
    score_grad = (probs * (prob_grad - center)).astype(jnp.bfloat16)
    dq = jnp.dot(score_grad, key, preferred_element_type=f32) * scale
    dq_ref[...] = dq.astype(dq_ref.dtype)
    dk_ref[...] = (cols_rows(score_grad, query) * scale).astype(dk_ref.dtype)
    dv_ref[...] = cols_rows(probs.astype(jnp.bfloat16), grad).astype(dv_ref.dtype)


def attend(grad, queries, enc_keys, enc_values, key_mask):
    rows, width = grad.shape
    reactions, _, length = key_mask.shape
    heads = width // HDIM
    block = pl.BlockSpec((length, HDIM), lambda r, h: (r, h))
    return pl.pallas_call(
        head_grads,
        grid=(reactions, heads),
        in_specs=[pl.BlockSpec((None, 1, length), lambda r, h: (r, 0, 0))] + [block] * 4,
        out_specs=[block] * 3,
        out_shape=[jax.ShapeDtypeStruct((rows, width), jnp.bfloat16)] * 3,
        cost_estimate=pl.CostEstimate(
            flops=10 * rows * length * width,
            bytes_accessed=14 * rows * width,
            transcendentals=rows * length * heads,
        ),
    )(key_mask, grad, queries, enc_keys, enc_values)


def project(grad_rows, weight_cols):
    return lax.dot_general(
        grad_rows, weight_cols, (((1,), (1,)), ((), ())), preferred_element_type=jnp.float32
    )


def per_device(out_grad, queries, enc_keys, enc_values, key_mask, weights):
    section = lax.axis_index("section")
    decoder = section == 1
    segment = lax.axis_index("segment")
    segments, shards = lax.axis_size("segment"), lax.axis_size("fsdp")
    micro_count, reactions, length, features = out_grad.shape
    shard_rows, width = weights.shape[2:]
    half = width // 2
    piece = length // segments
    rows = shards * reactions * length

    first_half = lax.ppermute(weights[0, 0, :, :half], "section", [(1, 0)])
    own_weight = jnp.where(decoder, weights[0, 0, :, half:], first_half)

    def own_half(array):
        return lax.dynamic_slice_in_dim(array, section * half, half, axis=array.ndim - 1)

    results = []
    for micro in range(micro_count):
        piece_grad = lax.dynamic_slice_in_dim(out_grad[micro], segment * piece, piece, axis=1)
        moved = lax.all_to_all(piece_grad, "fsdp", split_axis=2, concat_axis=0, tiled=True)
        spread = lax.all_gather(moved, "segment", axis=0)
        spread = spread.reshape(segments * shards * reactions * piece, shard_rows)
        partial = jnp.dot(spread, own_weight, preferred_element_type=jnp.float32)
        partial = partial.astype(jnp.bfloat16)
        partial = partial.reshape(segments, shards * reactions, piece, half).transpose(1, 0, 2, 3)
        ctx_grad = lax.psum_scatter(
            partial.reshape(rows, half), "fsdp", scatter_dimension=0, tiled=True
        )
        flat = (reactions * length, half)
        query_grad, key_grad, value_grad = attend(
            ctx_grad,
            own_half(queries[micro]).reshape(flat),
            own_half(enc_keys[micro]).reshape(flat),
            own_half(enc_values[micro]).reshape(flat),
            key_mask[micro][:, None, :],
        )
        all_values = lax.all_gather(value_grad, "fsdp", axis=0, tiled=True)
        received = lax.ppermute(
            jnp.where(decoder, key_grad, query_grad), "section", [(0, 1), (1, 0)]
        )
        first = jnp.where(decoder, received, key_grad)
        second = jnp.where(decoder, query_grad, received)
        all_first = lax.all_gather(
            jnp.concatenate([first, second], axis=1), "fsdp", axis=0, tiled=True
        )
        other_values = lax.ppermute(all_values, "section", [(1, 0)])

        def decoder_part():
            return project(all_first, weights[0, 1]).astype(jnp.bfloat16)

        def encoder_part():
            values = jnp.concatenate([all_values, other_values], axis=1)
            total = project(all_first, weights[0, 0]) + project(values, weights[0, 1])
            return total.astype(jnp.bfloat16)

        part = lax.cond(decoder, decoder_part, encoder_part)
        part = part.reshape(shards * reactions, segments, piece, shard_rows).transpose(1, 0, 2, 3)
        part = part.reshape(segments * shards * reactions * piece, shard_rows)
        summed = lax.psum_scatter(part, "segment", scatter_dimension=0, tiled=True)
        summed = summed.reshape(shards * reactions, piece, shard_rows)
        summed = lax.all_to_all(summed, "fsdp", split_axis=0, concat_axis=2, tiled=True)
        summed = lax.all_to_all(summed, "segment", split_axis=2, concat_axis=1, tiled=True)
        results.append(summed)
    return jnp.stack(results)[None]


def solution(mesh):
    return jax.shard_map(
        per_device,
        mesh=mesh,
        in_specs=(
            P(None, "fsdp", None, None),
            P(None, "fsdp", None, "segment"),
            P(None, "fsdp", None, "segment"),
            P(None, "fsdp", None, "segment"),
            P(None, "fsdp", None),
            P("section", None, "fsdp", "segment"),
        ),
        out_specs=P("section", None, "fsdp", None, "segment"),
        check_vma=False,
    )
```

time: 886 us -> 740 us (0.84)
  waiting for transfers between devices: 772 us -> 332 us
  other arithmetic: 3.26 us -> 145 us
  local copies, waits for them, and re-layouts: 46.7 us -> 114 us
  blocking collectives: 0 us -> 48.7 us
  starting transfers between devices: 5.27 us -> 25.7 us
  Pallas kernels: 0 us -> 13.1 us
    all_gather x1 -> x6, waiting for transfers between devices: 631 us -> 165 us  [the longest x2 125 us: per_device(): lax.all_gather(jnp.concatenate([first, second], axis=1), 'fsdp', axis=0,...]
    unnamed x0 -> x4, other arithmetic: none -> 138 us
    reduce_scatter x3 -> x4, waiting for transfers between devices: 36.4 us -> 96.1 us  [the longest x2 59.9 us: per_device(): summed = lax.psum_scatter(part, 'segment', scatter_dimension=0, tiled=True)]
    all_to_all x0 -> x16, local copies, waits for them, and re-layouts: none -> 52.6 us  [the longest x4 20.5 us: per_device(): lax.all_to_all(summed, 'fsdp', split_axis=0, concat_axis=2, tiled=True)]
    all_to_all x0 -> x2, blocking collectives: none -> 48.7 us  [per_device(): lax.all_to_all(piece_grad, 'fsdp', split_axis=2, concat_axis=0, tiled=True)]
    ppermute x4 -> x5, waiting for transfers between devices: 104 us -> 70.9 us  [the longest x1 52.5 us: per_device(): first_half = lax.ppermute(weights[0, 0, :, :half], 'section', [(1, 0)])]
    squeeze x1, local copies, waits for them, and re-layouts: 26.3 us -> 1.82 us  [per_device(): first_half = lax.ppermute(weights[0, 0, :, :half], 'section', [(1, 0)])]
    unnamed x16 -> x17, local copies, waits for them, and re-layouts: 3.99 us -> 26.5 us
  transfers between devices with their start and end apart: 8 -> 19, of which waited for: 6 -> 12; matrix products, arithmetic and copies ran while one was open for 7% -> 30% of each run, Pallas kernels for 0% -> 2%
where the time goes in v1:
time: 740 us; the launch traced here: 731 us
  waiting for transfers between devices  332 us (45%)
  other arithmetic  145 us (20%)
  local copies, waits for them, and re-layouts  114 us (15%)
  blocking collectives  48.7 us (7%)
  matrix products  37.6 us (5%)
  starting transfers between devices  25.7 us (3%)
  between operations  14.3 us (2%)
  Pallas kernels  13.1 us (2%)
    unnamed x4, other arithmetic  138 us
    all_gather x2, waiting for transfers between devices, per_device(): lax.all_gather(jnp.concatenate([first, second], axis=1), 'fsdp', axis=0,...  125 us
    reduce_scatter x2, waiting for transfers between devices, per_device(): summed = lax.psum_scatter(part, 'segment', scatter_dimension=0, tiled=True)  59.9 us
    ppermute x1, waiting for transfers between devices, per_device(): first_half = lax.ppermute(weights[0, 0, :, :half], 'section', [(1, 0)])  52.5 us
    all_to_all x2, blocking collectives, per_device(): lax.all_to_all(piece_grad, 'fsdp', split_axis=2, concat_axis=0, tiled=True)  48.7 us
    all_gather x2, waiting for transfers between devices, per_device(): all_values = lax.all_gather(value_grad, 'fsdp', axis=0, tiled=True)  39.3 us
    reduce_scatter x2, waiting for transfers between devices, per_device(): lax.psum_scatter(partial.reshape(rows, half), 'fsdp', scatter_dimension=0...  36.2 us
    unnamed x17, local copies, waits for them, and re-layouts  26.5 us
  transfers between devices with their start and end apart: 19, of which 12 were waited for; matrix products, arithmetic and copies ran while one was open for 30% of the time, Pallas kernels for 2%

profile of v1, /device:TPU:0, one launch (start us, length us, event | category | flops | bytes accessed | tf_op | source)
XLA Modules:
  0.0 731.1 jit_solution(10748256417712720120)
XLA Ops:
  21.2 34.4 %reduce = bf16[6144,64]{1,0:T(8,128)(2,1)} reduce(bf16[6144,1,64]{2,1,0:T(2,128)(2,1)S(1)} %bitcast.106, bf16[]{:T(256)} %broadcast), dimensions={1}, to_apply=%bitcast.88.reduce_sub_computation | reduce | bytes 1572866
  58.7 26.3 %all_to_all.96 = bf16[4,2,49152]{2,1,0:T(2,128)(2,1)} all-to-all(bf16[4,2,49152]{2,1,0:T(2,128)(2,1)S(1)} %reshape.96), channel_id=1, replica_groups=mesh['section'=2,'segment'=4,'fsdp'=4] {'fsdp'}, dimensions={0} | all-to-all | bytes 1572864 | tf_op jit(solution)/shard_map/all_to_all | solution.py:82
  96.5 6.7 copy.43
  103.2 34.4 %reduce.2 = bf16[6144,64]{1,0:T(8,128)(2,1)} reduce(bf16[6144,1,64]{2,1,0:T(2,128)(2,1)S(1)} %bitcast.107, bf16[]{:T(256)} %broadcast), dimensions={1}, to_apply=%bitcast.92.reduce_sub_computation | reduce | bytes 1572866
  140.7 22.4 %all_to_all.97 = bf16[4,2,49152]{2,1,0:T(2,128)(2,1)} all-to-all(bf16[4,2,49152]{2,1,0:T(2,128)(2,1)S(1)} %reshape.100), channel_id=1, replica_groups=mesh['section'=2,'segment'=4,'fsdp'=4] {'fsdp'}, dimensions={0} | all-to-all | bytes 1572864 | tf_op jit(solution)/shard_map/all_to_all | solution.py:82
  177.3 52.5 %collective-permute-done = bf16[1536,768]{1,0:T(8,128)(2,1)} collective-permute-done((bf16[1536,768]{1,0:T(8,128)(2,1)S(1)}, bf16[1536,768]{1,0:T(8,128)(2,1)}, u32[]{:S(2)}, u32[]{:S(2)}) %collective-permute-start) | collective-permute-done | bytes 2359328 | tf_op jit(solution)/shard_map/ppermute | solution.py:73
  249.2 22.0 %reduce-scatter.9.cloned.1.call-done.grad_ref = bf16[256,768]{1,0:T(8,128)(2,1)} async-done(((bf16[1024,768]{1,0:T(8,128)(2,1)}), bf16[256,768]{1,0:T(8,128)(2,1)}) %reduce-scatter.9.cloned.1.call-update) | async-done | bytes 393232 | tf_op jit(solution)/shard_map/reduce_scatter | solution.py:88
  280.4 9.2 %collective-permute-done.3 = bf16[256,768]{1,0:T(8,128)(2,1)S(1)} collective-permute-done((bf16[256,768]{1,0:T(8,128)(2,1)S(1)}, bf16[256,768]{1,0:T(8,128)(2,1)S(1)}, u32[]{:S(2)}, u32[]{:S(2)}) %collective-permute-start.3) | collective-permute-done | bytes 393248 | tf_op jit(solution)/shard_map/ppermute | solution.py:100
  293.4 14.2 %reduce-scatter.5.cloned.1.call-done.grad_ref = bf16[256,768]{1,0:T(8,128)(2,1)} async-done(((bf16[1024,768]{1,0:T(8,128)(2,1)}), bf16[256,768]{1,0:T(8,128)(2,1)}) %reduce-scatter.5.cloned.1.call-update) | async-done | bytes 393232 | tf_op jit(solution)/shard_map/reduce_scatter | solution.py:88
  316.8 9.2 %collective-permute-done.1 = bf16[256,768]{1,0:T(8,128)(2,1)S(1)} collective-permute-done((bf16[256,768]{1,0:T(8,128)(2,1)S(1)}, bf16[256,768]{1,0:T(8,128)(2,1)S(1)}, u32[]{:S(2)}, u32[]{:S(2)}) %collective-permute-start.1) | collective-permute-done | bytes 393248 | tf_op jit(solution)/shard_map/ppermute | solution.py:100
  328.1 16.9 %all-gather.15.cloned.1.call-done = bf16[1024,768]{1,0:T(8,128)(2,1)} async-done(((bf16[256,768]{1,0:T(8,128)(2,1)}), bf16[1024,768]{1,0:T(8,128)(2,1)}) %all-gather.15.cloned.1.call-update) | async-done | bytes 1572880 | tf_op jit(solution)/shard_map/all_gather | solution.py:99
  346.4 62.5 %all-gather.13.cloned.1.call-done = bf16[1024,1536]{1,0:T(8,128)(2,1)} async-done(((bf16[256,1536]{1,0:T(8,128)(2,1)}), bf16[1024,1536]{1,0:T(8,128)(2,1)}) %all-gather.13.cloned.1.call-update) | async-done | bytes 3145744 | tf_op jit(solution)/shard_map/all_gather | solution.py:105
  408.9 12.9 %conditional.5 = (bf16[1024,1536]{1,0:T(8,128)(2,1)S(1)}) conditional(s32[]{:T(128)} %convert_element_type.20, (bf16[1,2,1536,1536]{3,2,1,0:T(8,128)(2,1)}, bf16[1024,1536]{1,0:T(8,128)(2,1)}, bf16[1024,768]{1,0:T(8,128)(2,1)}, bf16[1024,768]{1,0:T(8,128)(2,1)S(1)}) %tuple.25, (bf16[1,2,1536,1536]{3,2,1,0:T(8,128)(2,1)}, ...), branch_computations={%region_5.6_spmd, %region_6.7_spmd} | conditional | flops 9673113600 | bytes 81788992
  408.9 7.6 %fusion.16 = f32[1024,1536]{1,0:T(8,128)S(1)} fusion(bf16[1,2,1536,1536]{3,2,1,0:T(8,128)(2,1)} %get-tuple-element.46, bf16[1024,768]{1,0:T(8,128)(2,1)S(1)} %get-tuple-element.48, bf16[1024,768]{1,0:T(8,128)(2,1)} %get-tuple-element.47), kind=kOutput, calls=%fused_computation.14 | convolution fusion | flops 4838129664 | bytes 14155776 | tf_op jit(solution)/shard_map/cond/branch_0_fun/dot_general | solution.py:57
  423.8 22.4 %all-gather.11.cloned.1.call-done = bf16[1024,768]{1,0:T(8,128)(2,1)} async-done(((bf16[256,768]{1,0:T(8,128)(2,1)}), bf16[1024,768]{1,0:T(8,128)(2,1)}) %all-gather.11.cloned.1.call-update) | async-done | bytes 1572880 | tf_op jit(solution)/shard_map/all_gather | solution.py:99
  447.5 62.7 %all-gather.9.cloned.1.call-done = bf16[1024,1536]{1,0:T(8,128)(2,1)} async-done(((bf16[256,1536]{1,0:T(8,128)(2,1)}), bf16[1024,1536]{1,0:T(8,128)(2,1)}) %all-gather.9.cloned.1.call-update) | async-done | bytes 3145744 | tf_op jit(solution)/shard_map/all_gather | solution.py:105
  510.2 13.1 %conditional.4 = (bf16[1024,1536]{1,0:T(8,128)(2,1)S(1)}) conditional(s32[]{:T(128)} %convert_element_type.20, (bf16[1,2,1536,1536]{3,2,1,0:T(8,128)(2,1)}, bf16[1024,1536]{1,0:T(8,128)(2,1)}, bf16[1024,768]{1,0:T(8,128)(2,1)}, bf16[1024,768]{1,0:T(8,128)(2,1)S(1)}) %tuple.23, (bf16[1,2,1536,1536]{3,2,1,0:T(8,128)(2,1)}, ...), branch_computations={%region_1.2_spmd, %region_2.3_spmd} | conditional | flops 9673113600 | bytes 81788992
  510.4 7.6 %fusion = f32[1024,1536]{1,0:T(8,128)S(1)} fusion(bf16[1,2,1536,1536]{3,2,1,0:T(8,128)(2,1)} %get-tuple-element.40, bf16[1024,768]{1,0:T(8,128)(2,1)S(1)} %get-tuple-element.42, bf16[1024,768]{1,0:T(8,128)(2,1)} %get-tuple-element.41), kind=kOutput, calls=%fused_computation | convolution fusion | flops 4838129664 | bytes 14155776 | tf_op jit(solution)/shard_map/cond/branch_0_fun/dot_general | solution.py:57
  525.4 24.0 %reduce-scatter.11.cloned.1.call-done = bf16[256,1536]{1,0:T(8,128)(2,1)} async-done(((bf16[1024,1536]{1,0:T(8,128)(2,1)}), bf16[256,1536]{1,0:T(8,128)(2,1)}) %reduce-scatter.11.cloned.1.call-update) | async-done | bytes 786448 | tf_op jit(solution)/shard_map/reduce_scatter | solution.py:121
  553.9 35.9 %reduce-scatter.7.cloned.1.call-done = bf16[256,1536]{1,0:T(8,128)(2,1)} async-done(((bf16[1024,1536]{1,0:T(8,128)(2,1)}), bf16[256,1536]{1,0:T(8,128)(2,1)}) %reduce-scatter.7.cloned.1.call-update) | async-done | bytes 786448 | tf_op jit(solution)/shard_map/reduce_scatter | solution.py:121
  596.0 8.3 %reshape.95 = bf16[1,64,6144]{1,0,2:T(2,128)(2,1)S(1)} reshape(bf16[1,64,4,1536]{1,3,2,0:T(8,128)(2,1)} %copy.63) | data formatting | bytes 1572864 | tf_op jit(solution)/shard_map/all_to_all | solution.py:123
  604.3 34.4 %reduce.1 = bf16[6144,64]{1,0:T(8,128)(2,1)} reduce(bf16[6144,1,64]{2,1,0:T(2,128)(2,1)S(1)} %bitcast.105, bf16[]{:T(256)} %broadcast), dimensions={1}, to_apply=%bitcast.90.reduce_sub_computation | reduce | bytes 1572866
  649.7 8.3 %reshape.94 = bf16[1,64,6144]{1,0,2:T(2,128)(2,1)S(1)} reshape(bf16[1,64,4,1536]{1,3,2,0:T(8,128)(2,1)} %copy.62) | data formatting | bytes 1572864 | tf_op jit(solution)/shard_map/all_to_all | solution.py:123
  657.9 34.4 %reduce.3 = bf16[6144,64]{1,0:T(8,128)(2,1)} reduce(bf16[6144,1,64]{2,1,0:T(2,128)(2,1)S(1)} %bitcast.104, bf16[]{:T(256)} %broadcast), dimensions={1}, to_apply=%bitcast.94.reduce_sub_computation | reduce | bytes 1572866
  (105 shorter events, 160.4 us)
Async XLA Ops:
  6.5 223.2 %all-gather.19.cloned.1.call-start = ((), (), s32[]{:S(2)}) async-start(), calls=%async_computation.19 | async-start | bytes 3932160 | tf_op jit(solution)/shard_map/all_gather | solution.py:83
  96.0 141.2 %all-gather.17.cloned.1.call-start = ((), (), s32[]{:S(2)}) async-start(), calls=%async_computation.18 | async-start | bytes 3932160 | tf_op jit(solution)/shard_map/all_gather | solution.py:83
  174.1 97.0 %reduce-scatter.9.cloned.1.call-start = ((), (), s32[]{:S(2)}) async-start(), calls=%async_computation.14 | async-start | bytes 1966080 | tf_op jit(solution)/shard_map/reduce_scatter | solution.py:88
  176.0 53.8 %collective-permute-start = (bf16[1536,768]{1,0:T(8,128)(2,1)S(1)}, bf16[1536,768]{1,0:T(8,128)(2,1)}, u32[]{:S(2)}, u32[]{:S(2)}) collective-permute-start(bf16[1536,768]{1,0:T(8,128)(2,1)S(1)} %slice_bitcast_fusion), channel_id=1, source_target_pairs={{16,0},{17,1},{18,2},{19,3},{20,4},{21,5},{22,6},{23,7},{24,8},{25... | collective-permute-start | bytes 7077896 | tf_op jit(solution)/shard_map/ppermute | solution.py:73
  237.0 70.6 %reduce-scatter.5.cloned.1.call-start = ((), (), s32[]{:S(2)}) async-start(), calls=%async_computation.10 | async-start | bytes 1966080 | tf_op jit(solution)/shard_map/reduce_scatter | solution.py:88
  244.5 100.6 %all-gather.15.cloned.1.call-start = ((), (), s32[]{:S(2)}) async-start(), calls=%async_computation.16 | async-start | bytes 1966080 | tf_op jit(solution)/shard_map/all_gather | solution.py:99
  277.7 131.2 %all-gather.13.cloned.1.call-start = ((), (), s32[]{:S(2)}) async-start(), calls=%async_computation.15 | async-start | bytes 3932160 | tf_op jit(solution)/shard_map/all_gather | solution.py:105
  278.9 10.7 %collective-permute-start.3 = (bf16[256,768]{1,0:T(8,128)(2,1)S(1)}, bf16[256,768]{1,0:T(8,128)(2,1)S(1)}, u32[]{:S(2)}, u32[]{:S(2)}) collective-permute-start(bf16[256,768]{1,0:T(8,128)(2,1)S(1)} %broadcast_select_fusion.2), channel_id=1, source_target_pairs={{0,16},{16,0},{1,17},{17,1},{2,18},{18,2},{3,19},{19,3},{4,20},{20... | collective-permute-start | bytes 1179656 | tf_op jit(solution)/shard_map/ppermute | solution.py:100
  291.6 154.6 %all-gather.11.cloned.1.call-start = ((), (), s32[]{:S(2)}) async-start(), calls=%async_computation.12 | async-start | bytes 1966080 | tf_op jit(solution)/shard_map/all_gather | solution.py:99
  314.2 196.0 %all-gather.9.cloned.1.call-start = ((), (), s32[]{:S(2)}) async-start(), calls=%async_computation.11 | async-start | bytes 3932160 | tf_op jit(solution)/shard_map/all_gather | solution.py:105
  315.3 10.7 %collective-permute-start.1 = (bf16[256,768]{1,0:T(8,128)(2,1)S(1)}, bf16[256,768]{1,0:T(8,128)(2,1)S(1)}, u32[]{:S(2)}, u32[]{:S(2)}) collective-permute-start(bf16[256,768]{1,0:T(8,128)(2,1)S(1)} %broadcast_select_fusion.5), channel_id=1, source_target_pairs={{0,16},{16,0},{1,17},{17,1},{2,18},{18,2},{3,19},{19,3},{4,20},{20... | collective-permute-start | bytes 1179656 | tf_op jit(solution)/shard_map/ppermute | solution.py:100
  328.1 221.3 %reduce-scatter.11.cloned.1.call-start = ((), (), s32[]{:S(2)}) async-start(), calls=%async_computation.17 | async-start | bytes 3932160 | tf_op jit(solution)/shard_map/reduce_scatter | solution.py:121
  345.1 63.8 %collective-permute-start.4 = (bf16[1024,768]{1,0:T(8,128)(2,1)}, bf16[1024,768]{1,0:T(8,128)(2,1)S(1)}, u32[]{:S(2)}, u32[]{:S(2)}) collective-permute-start(bf16[1024,768]{1,0:T(8,128)(2,1)} %all-gather.15.cloned.1.call-done), channel_id=1, source_target_pairs={{16,0},{17,1},{18,2},{19,3},{20,4},{21,5},{22,6},{23,7},{24,8},{25... | collective-permute-start | bytes 4718600 | tf_op jit(solution)/shard_map/ppermute | solution.py:108
  408.9 7.6 %copy-start.3 = (bf16[1,2,1536,1536]{3,2,1,0:T(8,128)(2,1)S(1)}, bf16[1,2,1536,1536]{3,2,1,0:T(8,128)(2,1)}, u32[]{:S(2)}) copy-start(bf16[1,2,1536,1536]{3,2,1,0:T(8,128)(2,1)} %get-tuple-element.46) | copy-start | bytes 28311556 | tf_op jit(solution)/shard_map/conditional.1
  408.9 7.6 %copy-start.6 = (bf16[1024,1536]{1,0:T(8,128)(2,1)S(1)}, bf16[1024,1536]{1,0:T(8,128)(2,1)}, u32[]{:S(2)}) copy-start(bf16[1024,1536]{1,0:T(8,128)(2,1)} %get-tuple-element.45) | copy-start | bytes 9437188 | tf_op jit(solution)/shard_map/conditional.1
  423.8 166.1 %reduce-scatter.7.cloned.1.call-start = ((), (), s32[]{:S(2)}) async-start(), calls=%async_computation.13 | async-start | bytes 3932160 | tf_op jit(solution)/shard_map/reduce_scatter | solution.py:121
  446.2 64.0 %collective-permute-start.2 = (bf16[1024,768]{1,0:T(8,128)(2,1)}, bf16[1024,768]{1,0:T(8,128)(2,1)S(1)}, u32[]{:S(2)}, u32[]{:S(2)}) collective-permute-start(bf16[1024,768]{1,0:T(8,128)(2,1)} %all-gather.11.cloned.1.call-done), channel_id=1, source_target_pairs={{16,0},{17,1},{18,2},{19,3},{20,4},{21,5},{22,6},{23,7},{24,8},{25... | collective-permute-start | bytes 4718600 | tf_op jit(solution)/shard_map/ppermute | solution.py:108
  510.4 7.6 %copy-start.4 = (bf16[1,2,1536,1536]{3,2,1,0:T(8,128)(2,1)S(1)}, bf16[1,2,1536,1536]{3,2,1,0:T(8,128)(2,1)}, u32[]{:S(2)}) copy-start(bf16[1,2,1536,1536]{3,2,1,0:T(8,128)(2,1)} %get-tuple-element.40) | copy-start | bytes 28311556 | tf_op jit(solution)/shard_map/conditional
  510.4 7.6 %copy-start.7 = (bf16[1024,1536]{1,0:T(8,128)(2,1)S(1)}, bf16[1024,1536]{1,0:T(8,128)(2,1)}, u32[]{:S(2)}) copy-start(bf16[1024,1536]{1,0:T(8,128)(2,1)} %get-tuple-element.39) | copy-start | bytes 9437188 | tf_op jit(solution)/shard_map/conditional
  549.4 40.5 %all-to-all-start.4 = ((bf16[4,64,1536]{2,1,0:T(8,128)(2,1)}), bf16[4,64,1536]{2,1,0:T(8,128)(2,1)S(1)}, u32[]{:S(2)}, u32[]{:S(2)}) async-start(bf16[4,64,1536]{2,1,0:T(8,128)(2,1)} %bitcast.125), calls=%async_computation.8 | async-start | bytes 1572864 | tf_op jit(solution)/shard_map/all_to_all | solution.py:123
  589.9 52.9 %all-to-all-start.1 = ((bf16[4,64,1536]{2,1,0:T(8,128)(2,1)}), bf16[4,64,1536]{2,1,0:T(8,128)(2,1)}, u32[]{:S(2)}, u32[]{:S(2)}) async-start(bf16[4,64,1536]{2,1,0:T(8,128)(2,1)} %bitcast.126), calls=%async_computation.3 | async-start | bytes 1572864 | tf_op jit(solution)/shard_map/all_to_all | solution.py:123
  642.8 53.6 %all-to-all-start.5 = ((bf16[4,2,49152]{2,1,0:T(2,128)(2,1)}), bf16[4,2,49152]{2,1,0:T(2,128)(2,1)}, u32[]{:S(2)}, u32[]{:S(2)}) async-start(bf16[4,2,49152]{2,1,0:T(2,128)(2,1)} %reshape.98), calls=%async_computation.9 | async-start | bytes 1572864 | tf_op jit(solution)/shard_map/all_to_all | solution.py:124
  696.4 15.9 %all-to-all-start.2 = ((bf16[4,2,49152]{2,1,0:T(2,128)(2,1)}), bf16[4,2,49152]{2,1,0:T(2,128)(2,1)}, u32[]{:S(2)}, u32[]{:S(2)}) async-start(bf16[4,2,49152]{2,1,0:T(2,128)(2,1)} %reshape.102), calls=%async_computation.4 | async-start | bytes 1572864 | tf_op jit(solution)/shard_map/all_to_all | solution.py:124
  720.0 2.5 copy-start
  (3 other events, 5.5 us)
Sparse Core Ops, SparseCore 0:
  96.1 27.6 all-gather.18
  174.2 27.6 all-gather.16
  237.1 33.9 reduce-scatter.8
  273.3 34.2 reduce-scatter.4
  309.0 36.0 all-gather.14
  346.5 62.3 all-gather.12
  410.5 35.7 all-gather.10
  447.8 62.3 all-gather.8
  512.7 36.5 reduce-scatter.10
  551.9 37.9 reduce-scatter.6

commit v2 on v1

--- a/solution.py
+++ b/solution.py
@@ -70,18 +70,33 @@
     piece = length // segments
     rows = shards * reactions * length
 
-    first_half = lax.ppermute(weights[0, 0, :, :half], "section", [(1, 0)])
-    own_weight = jnp.where(decoder, weights[0, 0, :, half:], first_half)
+    rows_cut = shard_rows // 2
+    sent_rows = [
+        lax.ppermute(weights[0, 0, :rows_cut, :half], "section", [(1, 0)]),
+        lax.ppermute(weights[0, 0, rows_cut:, :half], "section", [(1, 0)]),
+    ]
 
     def own_half(array):
         return lax.dynamic_slice_in_dim(array, section * half, half, axis=array.ndim - 1)
 
+    def across(array, axis):
+        return lax.all_to_all(array, axis, split_axis=0, concat_axis=0, tiled=True)
+
+    moved_list = []
+    for micro in range(micro_count):
+        piece_grad = lax.dynamic_slice_in_dim(out_grad[micro], segment * piece, piece, axis=1)
+        piece_grad = piece_grad.reshape(reactions * piece, shards, shard_rows).transpose(1, 0, 2)
+        moved_list.append(across(piece_grad, "fsdp"))
+    moved_list[0], sent_rows[0] = lax.optimization_barrier((moved_list[0], sent_rows[0]))
+    spread_list = [lax.all_gather(moved, "segment", axis=0) for moved in moved_list]
+    spread_list[0], sent_rows[1] = lax.optimization_barrier((spread_list[0], sent_rows[1]))
+    own_weight = jnp.where(
+        decoder, weights[0, 0, :, half:], jnp.concatenate(sent_rows, axis=0)
+    )
+
     results = []
     for micro in range(micro_count):
-        piece_grad = lax.dynamic_slice_in_dim(out_grad[micro], segment * piece, piece, axis=1)
-        moved = lax.all_to_all(piece_grad, "fsdp", split_axis=2, concat_axis=0, tiled=True)
-        spread = lax.all_gather(moved, "segment", axis=0)
-        spread = spread.reshape(segments * shards * reactions * piece, shard_rows)
+        spread = spread_list[micro].reshape(rows, shard_rows)
         partial = jnp.dot(spread, own_weight, preferred_element_type=jnp.float32)
         partial = partial.astype(jnp.bfloat16)
         partial = partial.reshape(segments, shards * reactions, piece, half).transpose(1, 0, 2, 3)
@@ -119,10 +134,12 @@
         part = part.reshape(shards * reactions, segments, piece, shard_rows).transpose(1, 0, 2, 3)
         part = part.reshape(segments * shards * reactions * piece, shard_rows)
         summed = lax.psum_scatter(part, "segment", scatter_dimension=0, tiled=True)
-        summed = summed.reshape(shards * reactions, piece, shard_rows)
-        summed = lax.all_to_all(summed, "fsdp", split_axis=0, concat_axis=2, tiled=True)
-        summed = lax.all_to_all(summed, "segment", split_axis=2, concat_axis=1, tiled=True)
-        results.append(summed)
+        summed = across(summed.reshape(shards, reactions * piece, shard_rows), "fsdp")
+        summed = summed.transpose(1, 0, 2).reshape(reactions * piece, segments, features // segments)
+        summed = across(summed.transpose(1, 0, 2), "segment")
+        summed = summed.reshape(segments, reactions, piece, features // segments)
+        summed = summed.transpose(1, 0, 2, 3)
+        results.append(summed.reshape(reactions, length, features // segments))
     return jnp.stack(results)[None]
 
 

time: 740 us -> 533 us (0.72)
  other arithmetic: 145 us -> 7.48 us
  local copies, waits for them, and re-layouts: 114 us -> 29.6 us
  blocking collectives: 48.7 us -> 75.5 us
    unnamed x4 -> x0, other arithmetic: 138 us -> none
    all_to_all x16 -> x0, local copies, waits for them, and re-layouts: 52.6 us -> none  [the longest x4 20.5 us: per_device(): lax.all_to_all(summed, 'fsdp', split_axis=0, concat_axis=2, tiled=True)]
    all_to_all x2 -> x4, blocking collectives: 48.7 us -> 75.5 us  [across(): return lax.all_to_all(array, axis, split_axis=0, concat_axis=0, tiled=True)]
    unnamed x17 -> x16, local copies, waits for them, and re-layouts: 26.5 us -> 2.65 us
    dynamic_slice x3 -> x1, local copies, waits for them, and re-layouts: 15.7 us -> 2.43 us  [per_device(): lax.dynamic_slice_in_dim(out_grad[micro], segment * piece, piece, axis=1)]
    ppermute x1 -> x2, waiting for transfers between devices: 52.5 us -> 40.1 us  [the longest x1 28.1 us: per_device(): lax.ppermute(weights[0, 0, rows_cut:, :half], 'section', [(1, 0)])]
    all_to_all x4 -> x2, starting transfers between devices: 17.8 us -> 10.9 us  [across(): return lax.all_to_all(array, axis, split_axis=0, concat_axis=0, tiled=True)]
  transfers between devices with their start and end apart: 19 -> 18, of which waited for: 12 -> 14; matrix products, arithmetic and copies ran while one was open for 30% -> 11% of each run, Pallas kernels for 2% -> 2%
where the time goes in v2:
time: 533 us; the launch traced here: 531 us
  waiting for transfers between devices  336 us (63%)
  blocking collectives  75.5 us (14%)
  matrix products  36.4 us (7%)
  local copies, waits for them, and re-layouts  29.6 us (6%)
  starting transfers between devices  19.5 us (4%)
  between operations  13.7 us (3%)
  Pallas kernels  13.1 us (2%)
  other arithmetic  7.48 us (1%)
    all_gather x2, waiting for transfers between devices, per_device(): lax.all_gather(jnp.concatenate([first, second], axis=1), 'fsdp', axis=0,...  125 us
    all_to_all x4, blocking collectives, across(): return lax.all_to_all(array, axis, split_axis=0, concat_axis=0, tiled=True)  75.5 us
    reduce_scatter x2, waiting for transfers between devices, per_device(): summed = lax.psum_scatter(part, 'segment', scatter_dimension=0, tiled=True)  60.2 us
    all_gather x2, waiting for transfers between devices, per_device(): all_values = lax.all_gather(value_grad, 'fsdp', axis=0, tiled=True)  39.4 us
    reduce_scatter x2, waiting for transfers between devices, per_device(): lax.psum_scatter(partial.reshape(rows, half), 'fsdp', scatter_dimension=0...  37.4 us
    ppermute x1, waiting for transfers between devices, per_device(): lax.ppermute(weights[0, 0, rows_cut:, :half], 'section', [(1, 0)])  28.1 us
    dot_general x4, matrix products, project(): lax.dot_general(grad_rows, weight_cols, (((1,), (1,)), ((), ())), preferr...  25.7 us
    ppermute x2, waiting for transfers between devices, per_device(): lax.ppermute(jnp.where(decoder, key_grad, query_grad), 'section', [(0, 1)...  18.4 us
  transfers between devices with their start and end apart: 18, of which 14 were waited for; matrix products, arithmetic and copies ran while one was open for 11% of the time, Pallas kernels for 2%

profile of v2, /device:TPU:0, one launch (start us, length us, event | category | flops | bytes accessed | tf_op | source)
XLA Modules:
  0.0 531.2 jit_solution(3639404481976873851)
XLA Ops:
  28.2 12.0 %collective-permute-done = bf16[768,768]{1,0:T(8,128)(2,1)} collective-permute-done((bf16[768,768]{1,0:T(8,128)(2,1)}, bf16[768,768]{1,0:T(8,128)(2,1)}, u32[]{:S(2)}, u32[]{:S(2)}) %collective-permute-start) | collective-permute-done | bytes 1179680 | tf_op jit(solution)/shard_map/ppermute | solution.py:75
  40.2 8.1 %all-to-all-done = bf16[4,64,1536]{2,1,0:T(8,128)(2,1)S(1)} async-done(((bf16[4,64,1536]{2,1,0:T(8,128)(2,1)}), bf16[4,64,1536]{2,1,0:T(8,128)(2,1)S(1)}, u32[]{:S(2)}, u32[]{:S(2)}) %all-to-all-start) | async-done | bytes 786464 | tf_op jit(solution)/shard_map/all_to_all | solution.py:83
  50.0 22.7 %all_to_all.30 = bf16[4,64,1536]{2,1,0:T(8,128)(2,1)} all-to-all(bf16[4,64,1536]{2,1,0:T(8,128)(2,1)S(1)} %copy.20), channel_id=1, replica_groups=mesh['section'=2,'segment'=4,'fsdp'=4] {'fsdp'}, dimensions={0} | all-to-all | bytes 1572864 | tf_op jit(solution)/shard_map/all_to_all | solution.py:83
  74.1 28.1 %collective-permute-done.1 = bf16[768,768]{1,0:T(8,128)(2,1)S(1)} collective-permute-done((bf16[768,768]{1,0:T(8,128)(2,1)S(1)}, bf16[768,768]{1,0:T(8,128)(2,1)S(1)}, u32[]{:S(2)}, u32[]{:S(2)}) %collective-permute-start.1) | collective-permute-done | bytes 1179680 | tf_op jit(solution)/shard_map/ppermute | solution.py:76
  102.3 6.8 %all-gather.19.cloned.1.call-done = bf16[16,64,1536]{2,1,0:T(8,128)(2,1)} async-done(((bf16[4,64,1536]{2,1,0:T(8,128)(2,1)}), bf16[16,64,1536]{2,1,0:T(8,128)(2,1)}) %all-gather.19.cloned.1.call-update) | async-done | bytes 3145744 | tf_op jit(solution)/shard_map/all_gather | solution.py:91
  128.2 23.2 %reduce-scatter.9.cloned.1.call-done.grad_ref = bf16[256,768]{1,0:T(8,128)(2,1)} async-done(((bf16[1024,768]{1,0:T(8,128)(2,1)}), bf16[256,768]{1,0:T(8,128)(2,1)}) %reduce-scatter.9.cloned.1.call-update) | async-done | bytes 393232 | tf_op jit(solution)/shard_map/reduce_scatter | solution.py:103
  151.4 6.5 %shard_map.65 = (bf16[256,768]{1,0:T(8,128)(2,1)}, bf16[256,768]{1,0:T(8,128)(2,1)}, bf16[256,768]{1,0:T(8,128)(2,1)}) custom-call(s32[1,1,256]{2,1,0:T(1,128)} %get-tuple-element.86.mask_ref, bf16[256,768]{1,0:T(8,128)(2,1)} %reduce-scatter.9.cloned.1.call-done.grad_ref, bf16[256,768]{1,0:T(8,128)(2,1)} %dynamic-slice_bitcast_fusion.2.query_ref, ...), custom_call_target="tpu_custom_call" | custom-call | flops 503316480 | bytes 2752512 | tf_op jit(solution)/shard_map/pallas_call | solution.py:42
  160.7 9.2 %collective-permute-done.4 = bf16[256,768]{1,0:T(8,128)(2,1)S(1)} collective-permute-done((bf16[256,768]{1,0:T(8,128)(2,1)S(1)}, bf16[256,768]{1,0:T(8,128)(2,1)S(1)}, u32[]{:S(2)}, u32[]{:S(2)}) %collective-permute-start.4) | collective-permute-done | bytes 393248 | tf_op jit(solution)/shard_map/ppermute | solution.py:115
  173.7 14.2 %reduce-scatter.5.cloned.1.call-done.grad_ref = bf16[256,768]{1,0:T(8,128)(2,1)} async-done(((bf16[1024,768]{1,0:T(8,128)(2,1)}), bf16[256,768]{1,0:T(8,128)(2,1)}) %reduce-scatter.5.cloned.1.call-update) | async-done | bytes 393232 | tf_op jit(solution)/shard_map/reduce_scatter | solution.py:103
  187.9 6.6 %shard_map.64 = (bf16[256,768]{1,0:T(8,128)(2,1)}, bf16[256,768]{1,0:T(8,128)(2,1)}, bf16[256,768]{1,0:T(8,128)(2,1)}) custom-call(s32[1,1,256]{2,1,0:T(1,128)} %get-tuple-element.85.mask_ref, bf16[256,768]{1,0:T(8,128)(2,1)} %reduce-scatter.5.cloned.1.call-done.grad_ref, bf16[256,768]{1,0:T(8,128)(2,1)} %dynamic-slice_bitcast_fusion.5.query_ref, ...), custom_call_target="tpu_custom_call" | custom-call | flops 503316480 | bytes 2752512 | tf_op jit(solution)/shard_map/pallas_call | solution.py:42
  197.1 9.2 %collective-permute-done.2 = bf16[256,768]{1,0:T(8,128)(2,1)S(1)} collective-permute-done((bf16[256,768]{1,0:T(8,128)(2,1)S(1)}, bf16[256,768]{1,0:T(8,128)(2,1)S(1)}, u32[]{:S(2)}, u32[]{:S(2)}) %collective-permute-start.2) | collective-permute-done | bytes 393248 | tf_op jit(solution)/shard_map/ppermute | solution.py:115
  208.5 16.9 %all-gather.15.cloned.1.call-done = bf16[1024,768]{1,0:T(8,128)(2,1)} async-done(((bf16[256,768]{1,0:T(8,128)(2,1)}), bf16[1024,768]{1,0:T(8,128)(2,1)}) %all-gather.15.cloned.1.call-update) | async-done | bytes 1572880 | tf_op jit(solution)/shard_map/all_gather | solution.py:114
  226.7 62.5 %all-gather.13.cloned.1.call-done = bf16[1024,1536]{1,0:T(8,128)(2,1)} async-done(((bf16[256,1536]{1,0:T(8,128)(2,1)}), bf16[1024,1536]{1,0:T(8,128)(2,1)}) %all-gather.13.cloned.1.call-update) | async-done | bytes 3145744 | tf_op jit(solution)/shard_map/all_gather | solution.py:120
  289.2 12.9 %conditional.5 = (bf16[1024,1536]{1,0:T(8,128)(2,1)S(1)}) conditional(s32[]{:T(128)} %convert_element_type.20, (bf16[1,2,1536,1536]{3,2,1,0:T(8,128)(2,1)}, bf16[1024,1536]{1,0:T(8,128)(2,1)}, bf16[1024,768]{1,0:T(8,128)(2,1)}, bf16[1024,768]{1,0:T(8,128)(2,1)S(1)}) %tuple.29, (bf16[1,2,1536,1536]{3,2,1,0:T(8,128)(2,1)}, ...), branch_computations={%region_5.6_spmd, %region_6.7_spmd} | conditional | flops 9673113600 | bytes 81788992
  289.2 7.6 %fusion.16 = f32[1024,1536]{1,0:T(8,128)S(1)} fusion(bf16[1,2,1536,1536]{3,2,1,0:T(8,128)(2,1)} %get-tuple-element.46, bf16[1024,768]{1,0:T(8,128)(2,1)S(1)} %get-tuple-element.48, bf16[1024,768]{1,0:T(8,128)(2,1)} %get-tuple-element.47), kind=kOutput, calls=%fused_computation.14 | convolution fusion | flops 4838129664 | bytes 14155776 | tf_op jit(solution)/shard_map/cond/branch_0_fun/dot_general | solution.py:57
  304.2 22.4 %all-gather.11.cloned.1.call-done = bf16[1024,768]{1,0:T(8,128)(2,1)} async-done(((bf16[256,768]{1,0:T(8,128)(2,1)}), bf16[1024,768]{1,0:T(8,128)(2,1)}) %all-gather.11.cloned.1.call-update) | async-done | bytes 1572880 | tf_op jit(solution)/shard_map/all_gather | solution.py:114
  327.9 62.7 %all-gather.9.cloned.1.call-done = bf16[1024,1536]{1,0:T(8,128)(2,1)} async-done(((bf16[256,1536]{1,0:T(8,128)(2,1)}), bf16[1024,1536]{1,0:T(8,128)(2,1)}) %all-gather.9.cloned.1.call-update) | async-done | bytes 3145744 | tf_op jit(solution)/shard_map/all_gather | solution.py:120
  390.6 12.9 %conditional.4 = (bf16[1024,1536]{1,0:T(8,128)(2,1)S(1)}) conditional(s32[]{:T(128)} %convert_element_type.20, (bf16[1,2,1536,1536]{3,2,1,0:T(8,128)(2,1)}, bf16[1024,1536]{1,0:T(8,128)(2,1)}, bf16[1024,768]{1,0:T(8,128)(2,1)}, bf16[1024,768]{1,0:T(8,128)(2,1)S(1)}) %tuple.27, (bf16[1,2,1536,1536]{3,2,1,0:T(8,128)(2,1)}, ...), branch_computations={%region_1.2_spmd, %region_2.3_spmd} | conditional | flops 9673113600 | bytes 81788992
  390.6 7.6 %fusion = f32[1024,1536]{1,0:T(8,128)S(1)} fusion(bf16[1,2,1536,1536]{3,2,1,0:T(8,128)(2,1)} %get-tuple-element.40, bf16[1024,768]{1,0:T(8,128)(2,1)S(1)} %get-tuple-element.42, bf16[1024,768]{1,0:T(8,128)(2,1)} %get-tuple-element.41), kind=kOutput, calls=%fused_computation | convolution fusion | flops 4838129664 | bytes 14155776 | tf_op jit(solution)/shard_map/cond/branch_0_fun/dot_general | solution.py:57
  405.4 24.3 %reduce-scatter.11.cloned.1.call-done = bf16[256,1536]{1,0:T(8,128)(2,1)} async-done(((bf16[1024,1536]{1,0:T(8,128)(2,1)}), bf16[256,1536]{1,0:T(8,128)(2,1)}) %reduce-scatter.11.cloned.1.call-update) | async-done | bytes 786448 | tf_op jit(solution)/shard_map/reduce_scatter | solution.py:136
  434.3 35.9 %reduce-scatter.7.cloned.1.call-done = bf16[256,1536]{1,0:T(8,128)(2,1)} async-done(((bf16[1024,1536]{1,0:T(8,128)(2,1)}), bf16[256,1536]{1,0:T(8,128)(2,1)}) %reduce-scatter.7.cloned.1.call-update) | async-done | bytes 786448 | tf_op jit(solution)/shard_map/reduce_scatter | solution.py:136
  470.2 24.7 %all_to_all.31 = bf16[4,64,1536]{2,1,0:T(8,128)(2,1)S(1)} all-to-all(bf16[4,64,1536]{2,1,0:T(8,128)(2,1)} %bitcast.94), channel_id=1, replica_groups=mesh['section'=2,'segment'=4,'fsdp'=4] {'fsdp'}, dimensions={0} | all-to-all | bytes 1572864 | tf_op jit(solution)/shard_map/all_to_all | solution.py:83
  495.0 14.1 %all_to_all.32 = bf16[4,64,1536]{2,1,0:T(8,128)(2,1)S(1)} all-to-all(bf16[4,64,1536]{2,1,0:T(8,128)(2,1)S(1)} %all-to-all-done.4), channel_id=1, replica_groups=mesh['section'=2,'segment'=4,'fsdp'=4] {'segment'}, dimensions={0} | all-to-all | bytes 1572864 | tf_op jit(solution)/shard_map/all_to_all | solution.py:83
  509.0 14.1 %all_to_all.33 = bf16[4,64,1536]{2,1,0:T(8,128)(2,1)S(1)} all-to-all(bf16[4,64,1536]{2,1,0:T(8,128)(2,1)S(1)} %all_to_all.31), channel_id=1, replica_groups=mesh['section'=2,'segment'=4,'fsdp'=4] {'segment'}, dimensions={0} | all-to-all | bytes 1572864 | tf_op jit(solution)/shard_map/all_to_all | solution.py:83
  (86 shorter events, 78.0 us)
Async XLA Ops:
  9.7 30.5 %collective-permute-start = (bf16[768,768]{1,0:T(8,128)(2,1)}, bf16[768,768]{1,0:T(8,128)(2,1)}, u32[]{:S(2)}, u32[]{:S(2)}) collective-permute-start(bf16[768,768]{1,0:T(8,128)(2,1)} %get-tuple-element.72), channel_id=1, source_target_pairs={{16,0},{17,1},{18,2},{19,3},{20,4},{21,5},{22,6},{23,7},{24,8},{25... | collective-permute-start | bytes 3538952 | tf_op jit(solution)/shard_map/ppermute | solution.py:75
  18.5 30.8 %copy-start.1 = (bf16[1,1,64,6144]{3,2,1,0:T(8,128)(2,1)S(1)}, bf16[1,1,64,6144]{3,2,1,0:T(8,128)(2,1)}, u32[]{:S(2)}) copy-start(bf16[1,1,64,6144]{3,2,1,0:T(8,128)(2,1)} %get-tuple-element.87) | copy-start | bytes 2359300
  21.9 26.4 %all-to-all-start = ((bf16[4,64,1536]{2,1,0:T(8,128)(2,1)}), bf16[4,64,1536]{2,1,0:T(8,128)(2,1)S(1)}, u32[]{:S(2)}, u32[]{:S(2)}) async-start(bf16[4,64,1536]{2,1,0:T(8,128)(2,1)} %copy.17), calls=%async_computation | async-start | bytes 1572864 | tf_op jit(solution)/shard_map/all_to_all | solution.py:83
  28.2 74.0 %all-gather.17.cloned.1.call-start = ((), (), s32[]{:S(2)}) async-start(), calls=%async_computation.18 | async-start | bytes 3932160 | tf_op jit(solution)/shard_map/all_gather | solution.py:91
  48.3 24.5 %copy-start.4 = (bf16[768,768]{1,0:T(8,128)(2,1)S(1)}, bf16[768,768]{1,0:T(8,128)(2,1)}, u32[]{:S(2)}) copy-start(bf16[768,768]{1,0:T(8,128)(2,1)} %get-tuple-element.71) | copy-start | bytes 3538948
  49.3 59.8 %all-gather.19.cloned.1.call-start = ((), (), s32[]{:S(2)}) async-start(), calls=%async_computation.19 | async-start | bytes 3932160 | tf_op jit(solution)/shard_map/all_gather | solution.py:91
  72.8 78.6 %reduce-scatter.9.cloned.1.call-start = ((), (), s32[]{:S(2)}) async-start(), calls=%async_computation.14 | async-start | bytes 1966080 | tf_op jit(solution)/shard_map/reduce_scatter | solution.py:103
  72.8 29.4 %collective-permute-start.1 = (bf16[768,768]{1,0:T(8,128)(2,1)S(1)}, bf16[768,768]{1,0:T(8,128)(2,1)S(1)}, u32[]{:S(2)}, u32[]{:S(2)}) collective-permute-start(bf16[768,768]{1,0:T(8,128)(2,1)S(1)} %copy-done.4), channel_id=1, source_target_pairs={{16,0},{17,1},{18,2},{19,3},{20,4},{21,5},{22,6},{23,7},{24,8},{25... | collective-permute-start | bytes 3538952 | tf_op jit(solution)/shard_map/ppermute | solution.py:76
  116.0 71.9 %reduce-scatter.5.cloned.1.call-start = ((), (), s32[]{:S(2)}) async-start(), calls=%async_computation.10 | async-start | bytes 1966080 | tf_op jit(solution)/shard_map/reduce_scatter | solution.py:103
  123.5 102.0 %all-gather.15.cloned.1.call-start = ((), (), s32[]{:S(2)}) async-start(), calls=%async_computation.16 | async-start | bytes 1966080 | tf_op jit(solution)/shard_map/all_gather | solution.py:114
  158.0 131.3 %all-gather.13.cloned.1.call-start = ((), (), s32[]{:S(2)}) async-start(), calls=%async_computation.15 | async-start | bytes 3932160 | tf_op jit(solution)/shard_map/all_gather | solution.py:120
  159.2 10.7 %collective-permute-start.4 = (bf16[256,768]{1,0:T(8,128)(2,1)S(1)}, bf16[256,768]{1,0:T(8,128)(2,1)S(1)}, u32[]{:S(2)}, u32[]{:S(2)}) collective-permute-start(bf16[256,768]{1,0:T(8,128)(2,1)S(1)} %broadcast_select_fusion.2), channel_id=1, source_target_pairs={{0,16},{16,0},{1,17},{17,1},{2,18},{18,2},{3,19},{19,3},{4,20},{20... | collective-permute-start | bytes 1179656 | tf_op jit(solution)/shard_map/ppermute | solution.py:115
  171.9 154.7 %all-gather.11.cloned.1.call-start = ((), (), s32[]{:S(2)}) async-start(), calls=%async_computation.12 | async-start | bytes 1966080 | tf_op jit(solution)/shard_map/all_gather | solution.py:114
  194.5 196.1 %all-gather.9.cloned.1.call-start = ((), (), s32[]{:S(2)}) async-start(), calls=%async_computation.11 | async-start | bytes 3932160 | tf_op jit(solution)/shard_map/all_gather | solution.py:120
  195.6 10.8 %collective-permute-start.2 = (bf16[256,768]{1,0:T(8,128)(2,1)S(1)}, bf16[256,768]{1,0:T(8,128)(2,1)S(1)}, u32[]{:S(2)}, u32[]{:S(2)}) collective-permute-start(bf16[256,768]{1,0:T(8,128)(2,1)S(1)} %broadcast_select_fusion.5), channel_id=1, source_target_pairs={{0,16},{16,0},{1,17},{17,1},{2,18},{18,2},{3,19},{19,3},{4,20},{20... | collective-permute-start | bytes 1179656 | tf_op jit(solution)/shard_map/ppermute | solution.py:115
  208.4 221.3 %reduce-scatter.11.cloned.1.call-start = ((), (), s32[]{:S(2)}) async-start(), calls=%async_computation.17 | async-start | bytes 3932160 | tf_op jit(solution)/shard_map/reduce_scatter | solution.py:136
  225.4 63.8 %collective-permute-start.5 = (bf16[1024,768]{1,0:T(8,128)(2,1)}, bf16[1024,768]{1,0:T(8,128)(2,1)S(1)}, u32[]{:S(2)}, u32[]{:S(2)}) collective-permute-start(bf16[1024,768]{1,0:T(8,128)(2,1)} %all-gather.15.cloned.1.call-done), channel_id=1, source_target_pairs={{16,0},{17,1},{18,2},{19,3},{20,4},{21,5},{22,6},{23,7},{24,8},{25... | collective-permute-start | bytes 4718600 | tf_op jit(solution)/shard_map/ppermute | solution.py:123
  289.2 7.6 %copy-start.5 = (bf16[1,2,1536,1536]{3,2,1,0:T(8,128)(2,1)S(1)}, bf16[1,2,1536,1536]{3,2,1,0:T(8,128)(2,1)}, u32[]{:S(2)}) copy-start(bf16[1,2,1536,1536]{3,2,1,0:T(8,128)(2,1)} %get-tuple-element.46) | copy-start | bytes 28311556 | tf_op jit(solution)/shard_map/conditional.1
  289.2 7.6 %copy-start.8 = (bf16[1024,1536]{1,0:T(8,128)(2,1)S(1)}, bf16[1024,1536]{1,0:T(8,128)(2,1)}, u32[]{:S(2)}) copy-start(bf16[1024,1536]{1,0:T(8,128)(2,1)} %get-tuple-element.45) | copy-start | bytes 9437188 | tf_op jit(solution)/shard_map/conditional.1
  304.1 166.1 %reduce-scatter.7.cloned.1.call-start = ((), (), s32[]{:S(2)}) async-start(), calls=%async_computation.13 | async-start | bytes 3932160 | tf_op jit(solution)/shard_map/reduce_scatter | solution.py:136
  326.6 64.0 %collective-permute-start.3 = (bf16[1024,768]{1,0:T(8,128)(2,1)}, bf16[1024,768]{1,0:T(8,128)(2,1)S(1)}, u32[]{:S(2)}, u32[]{:S(2)}) collective-permute-start(bf16[1024,768]{1,0:T(8,128)(2,1)} %all-gather.11.cloned.1.call-done), channel_id=1, source_target_pairs={{16,0},{17,1},{18,2},{19,3},{20,4},{21,5},{22,6},{23,7},{24,8},{25... | collective-permute-start | bytes 4718600 | tf_op jit(solution)/shard_map/ppermute | solution.py:123
  390.6 7.6 %copy-start.6 = (bf16[1,2,1536,1536]{3,2,1,0:T(8,128)(2,1)S(1)}, bf16[1,2,1536,1536]{3,2,1,0:T(8,128)(2,1)}, u32[]{:S(2)}) copy-start(bf16[1,2,1536,1536]{3,2,1,0:T(8,128)(2,1)} %get-tuple-element.40) | copy-start | bytes 28311556 | tf_op jit(solution)/shard_map/conditional
  390.6 7.6 %copy-start.9 = (bf16[1024,1536]{1,0:T(8,128)(2,1)S(1)}, bf16[1024,1536]{1,0:T(8,128)(2,1)}, u32[]{:S(2)}) copy-start(bf16[1024,1536]{1,0:T(8,128)(2,1)} %get-tuple-element.39) | copy-start | bytes 9437188 | tf_op jit(solution)/shard_map/conditional
  429.7 40.5 %all-to-all-start.4 = ((bf16[4,64,1536]{2,1,0:T(8,128)(2,1)}), bf16[4,64,1536]{2,1,0:T(8,128)(2,1)S(1)}, u32[]{:S(2)}, u32[]{:S(2)}) async-start(bf16[4,64,1536]{2,1,0:T(8,128)(2,1)} %bitcast.93), calls=%async_computation.8 | async-start | bytes 1572864 | tf_op jit(solution)/shard_map/all_to_all | solution.py:83
  (6 other events, 15.6 us)
Sparse Core Ops, SparseCore 0:
  49.4 29.4 all-gather.16
  80.5 28.5 all-gather.18
  116.1 35.2 reduce-scatter.8
  153.6 34.2 reduce-scatter.4
  189.3 36.0 all-gather.14
  226.8 62.3 all-gather.12
  290.8 35.7 all-gather.10
  328.1 62.3 all-gather.8
  393.1 36.5 reduce-scatter.10
  432.3 37.9 reduce-scatter.6

commit v3 on v2

--- a/solution.py
+++ b/solution.py
@@ -82,27 +82,37 @@
     def across(array, axis):
         return lax.all_to_all(array, axis, split_axis=0, concat_axis=0, tiled=True)
 
+    pieces = []
+    for micro in range(micro_count):
+        piece_grad = lax.dynamic_slice_in_dim(out_grad[micro], segment * piece, piece, axis=1)
+        pieces.append(
+            piece_grad.reshape(reactions * piece, shards, shard_rows).transpose(1, 0, 2)
+        )
     moved_list = []
     for micro in range(micro_count):
-        piece_grad = lax.dynamic_slice_in_dim(out_grad[micro], segment * piece, piece, axis=1)
-        piece_grad = piece_grad.reshape(reactions * piece, shards, shard_rows).transpose(1, 0, 2)
-        moved_list.append(across(piece_grad, "fsdp"))
-    moved_list[0], sent_rows[0] = lax.optimization_barrier((moved_list[0], sent_rows[0]))
-    spread_list = [lax.all_gather(moved, "segment", axis=0) for moved in moved_list]
-    spread_list[0], sent_rows[1] = lax.optimization_barrier((spread_list[0], sent_rows[1]))
+        moved_list.append(across(pieces[micro], "fsdp"))
+        if micro < 2:
+            moved_list[micro], sent_rows[micro] = lax.optimization_barrier(
+                (moved_list[micro], sent_rows[micro])
+            )
     own_weight = jnp.where(
         decoder, weights[0, 0, :, half:], jnp.concatenate(sent_rows, axis=0)
     )
 
-    results = []
+    grads_list = []
     for micro in range(micro_count):
-        spread = spread_list[micro].reshape(rows, shard_rows)
-        partial = jnp.dot(spread, own_weight, preferred_element_type=jnp.float32)
-        partial = partial.astype(jnp.bfloat16)
+        moved = moved_list[micro]
+        if micro == 0:
+            spread = lax.all_gather(moved, "segment", axis=0)
+        else:
+            moved, _ = lax.optimization_barrier((moved, partial))
+            spread = across(jnp.broadcast_to(moved[None], (segments,) + moved.shape), "segment")
+        partial = jnp.dot(
+            spread.reshape(rows, shard_rows), own_weight, preferred_element_type=jnp.float32
+        ).astype(jnp.bfloat16)
         partial = partial.reshape(segments, shards * reactions, piece, half).transpose(1, 0, 2, 3)
-        ctx_grad = lax.psum_scatter(
-            partial.reshape(rows, half), "fsdp", scatter_dimension=0, tiled=True
-        )
+        partial = partial.reshape(rows, half)
+        ctx_grad = lax.psum_scatter(partial, "fsdp", scatter_dimension=0, tiled=True)
         flat = (reactions * length, half)
         query_grad, key_grad, value_grad = attend(
             ctx_grad,
@@ -111,29 +121,50 @@
             own_half(enc_values[micro]).reshape(flat),
             key_mask[micro][:, None, :],
         )
-        all_values = lax.all_gather(value_grad, "fsdp", axis=0, tiled=True)
         received = lax.ppermute(
             jnp.where(decoder, key_grad, query_grad), "section", [(0, 1), (1, 0)]
         )
         first = jnp.where(decoder, received, key_grad)
         second = jnp.where(decoder, query_grad, received)
+        grads_list.append((first, second, value_grad))
+
+    gathered_list = []
+    for micro in range(micro_count):
+        first, second, value_grad = grads_list[micro]
+        all_values = lax.all_gather(value_grad, "fsdp", axis=0, tiled=True)
         all_first = lax.all_gather(
             jnp.concatenate([first, second], axis=1), "fsdp", axis=0, tiled=True
         )
         other_values = lax.ppermute(all_values, "section", [(1, 0)])
+        gathered_list.append((all_first, all_values, other_values))
+
+    results = []
+    for micro in range(micro_count):
+        all_first, all_values, other_values = gathered_list[micro]
+
+        def no_values():
+            return jnp.zeros((rows, shard_rows), jnp.float32)
+
+        def values_part():
+            values = jnp.concatenate([all_values, other_values], axis=1)
+            return project(values, weights[0, 1])
+
+        from_values = lax.cond(decoder, no_values, values_part)
+        if micro > 0:
+            all_first, results[-1], from_values = lax.optimization_barrier(
+                (all_first, results[-1], from_values)
+            )
 
         def decoder_part():
             return project(all_first, weights[0, 1]).astype(jnp.bfloat16)
 
         def encoder_part():
-            values = jnp.concatenate([all_values, other_values], axis=1)
-            total = project(all_first, weights[0, 0]) + project(values, weights[0, 1])
-            return total.astype(jnp.bfloat16)
+            return (project(all_first, weights[0, 0]) + from_values).astype(jnp.bfloat16)
 
         part = lax.cond(decoder, decoder_part, encoder_part)
         part = part.reshape(shards * reactions, segments, piece, shard_rows).transpose(1, 0, 2, 3)
-        part = part.reshape(segments * shards * reactions * piece, shard_rows)
-        summed = lax.psum_scatter(part, "segment", scatter_dimension=0, tiled=True)
+        part = across(part.reshape(segments, shards * reactions * piece, shard_rows), "segment")
+        summed = jnp.sum(part.astype(jnp.float32), axis=0).astype(jnp.bfloat16)
         summed = across(summed.reshape(shards, reactions * piece, shard_rows), "fsdp")
         summed = summed.transpose(1, 0, 2).reshape(reactions * piece, segments, features // segments)
         summed = across(summed.transpose(1, 0, 2), "segment")

time: 533 us -> 497 us (0.932)
  waiting for transfers between devices: 336 us -> 200 us
  blocking collectives: 75.5 us -> 156 us
  matrix products: 36.4 us -> 48 us
  starting transfers between devices: 19.5 us -> 27.1 us
    all_gather x2, waiting for transfers between devices: 125 us -> 13.7 us  [per_device(): lax.all_gather(jnp.concatenate([first, second], axis=1), 'fsdp', axis=0,...]
    reduce_scatter x4 -> x2, waiting for transfers between devices: 97.6 us -> 7.91 us  [per_device(): lax.psum_scatter(partial, 'fsdp', scatter_dimension=0, tiled=True)]
    all_to_all x4 -> x5, blocking collectives: 75.5 us -> 156 us  [across(): return lax.all_to_all(array, axis, split_axis=0, concat_axis=0, tiled=True)]
    all_to_all x2 -> x4, waiting for transfers between devices: 8.11 us -> 73.9 us  [across(): return lax.all_to_all(array, axis, split_axis=0, concat_axis=0, tiled=True)]
    ppermute x2, waiting for transfers between devices: 18.4 us -> 51.8 us  [per_device(): lax.ppermute(jnp.where(decoder, key_grad, query_grad), 'section', [(0, 1)...]
    ppermute x1, waiting for transfers between devices: 28.1 us -> 9.31 us  [per_device(): lax.ppermute(weights[0, 0, rows_cut:, :half], 'section', [(1, 0)])]
    dot_general x4, matrix products: 25.7 us -> 37 us  [project(): lax.dot_general(grad_rows, weight_cols, (((1,), (1,)), ((), ())), preferr...]
    all_gather x2, waiting for transfers between devices: 39.4 us -> 30.9 us  [per_device(): all_values = lax.all_gather(value_grad, 'fsdp', axis=0, tiled=True)]
  transfers between devices with their start and end apart: 18 -> 17, of which waited for: 14 -> 11; matrix products, arithmetic and copies ran while one was open for 11% -> 11% of each run, Pallas kernels for 2% -> 3%
where the time goes in v3:
time: 497 us; the launch traced here: 495 us
  waiting for transfers between devices  200 us (40%)
  blocking collectives  156 us (31%)
  matrix products  48 us (10%)
  starting transfers between devices  27.1 us (5%)
  local copies, waits for them, and re-layouts  25.9 us (5%)
  between operations  13.7 us (3%)
  Pallas kernels  13.2 us (3%)
  other arithmetic  10.5 us (2%)
    all_to_all x5, blocking collectives, across(): return lax.all_to_all(array, axis, split_axis=0, concat_axis=0, tiled=True)  156 us
    all_to_all x4, waiting for transfers between devices, across(): return lax.all_to_all(array, axis, split_axis=0, concat_axis=0, tiled=True)  73.9 us
    ppermute x2, waiting for transfers between devices, per_device(): lax.ppermute(jnp.where(decoder, key_grad, query_grad), 'section', [(0, 1)...  51.8 us
    dot_general x4, matrix products, project(): lax.dot_general(grad_rows, weight_cols, (((1,), (1,)), ((), ())), preferr...  37 us
    all_gather x2, waiting for transfers between devices, per_device(): all_values = lax.all_gather(value_grad, 'fsdp', axis=0, tiled=True)  30.9 us
    all_to_all x4, starting transfers between devices, across(): return lax.all_to_all(array, axis, split_axis=0, concat_axis=0, tiled=True)  18.8 us
    all_gather x2, waiting for transfers between devices, per_device(): lax.all_gather(jnp.concatenate([first, second], axis=1), 'fsdp', axis=0,...  13.7 us
    pallas_call x2, Pallas kernels, attend(): pl.pallas_call(head_grads, grid=(reactions, heads), in_specs=[pl.BlockSpe...  13.2 us
  transfers between devices with their start and end apart: 17, of which 11 were waited for; matrix products, arithmetic and copies ran while one was open for 11% of the time, Pallas kernels for 3%

profile of v3, /device:TPU:0, one launch (start us, length us, event | category | flops | bytes accessed | tf_op | source)
XLA Modules:
  0.0 495.2 jit_solution(10421533927555272905)
XLA Ops:
  27.8 16.0 %all-to-all-done.1 = bf16[4,64,1536]{2,1,0:T(8,128)(2,1)S(1)} async-done(((bf16[4,64,1536]{2,1,0:T(8,128)(2,1)}), bf16[4,64,1536]{2,1,0:T(8,128)(2,1)S(1)}, u32[]{:S(2)}, u32[]{:S(2)}) %all-to-all-start.1) | async-done | bytes 786464 | tf_op jit(solution)/shard_map/all_to_all | solution.py:83
  43.8 12.4 %collective-permute-done.1 = bf16[768,768]{1,0:T(8,128)(2,1)} collective-permute-done((bf16[768,768]{1,0:T(8,128)(2,1)}, bf16[768,768]{1,0:T(8,128)(2,1)}, u32[]{:S(2)}, u32[]{:S(2)}) %collective-permute-start.1) | collective-permute-done | bytes 1179680 | tf_op jit(solution)/shard_map/ppermute | solution.py:75
  63.9 17.3 %all-to-all-done = bf16[4,64,1536]{2,1,0:T(8,128)(2,1)S(1)} async-done(((bf16[4,64,1536]{2,1,0:T(8,128)(2,1)}), bf16[4,64,1536]{2,1,0:T(8,128)(2,1)S(1)}, u32[]{:S(2)}, u32[]{:S(2)}) %all-to-all-start) | async-done | bytes 786464 | tf_op jit(solution)/shard_map/all_to_all | solution.py:83
  81.2 9.3 %collective-permute-done = bf16[768,768]{1,0:T(8,128)(2,1)} collective-permute-done((bf16[768,768]{1,0:T(8,128)(2,1)S(1)}, bf16[768,768]{1,0:T(8,128)(2,1)}, u32[]{:S(2)}, u32[]{:S(2)}) %collective-permute-start) | collective-permute-done | bytes 1179680 | tf_op jit(solution)/shard_map/ppermute | solution.py:76
  98.1 39.5 %all_to_all.45 = bf16[4,4,64,1536]{3,2,1,0:T(8,128)(2,1)S(1)} all-to-all(bf16[4,4,64,1536]{3,2,1,0:T(8,128)(2,1)S(1)} %broadcast_in_dim.4), channel_id=1, replica_groups=mesh['section'=2,'segment'=4,'fsdp'=4] {'segment'}, dimensions={0} | all-to-all | bytes 6291456 | tf_op jit(solution)/shard_map/all_to_all | solution.py:83
  148.7 6.7 %shard_map.65 = (bf16[256,768]{1,0:T(8,128)(2,1)}, bf16[256,768]{1,0:T(8,128)(2,1)}, bf16[256,768]{1,0:T(8,128)(2,1)}) custom-call(s32[1,1,256]{2,1,0:T(1,128)} %get-tuple-element.111.mask_ref, bf16[256,768]{1,0:T(8,128)(2,1)} %reduce-scatter.5.cloned.1.call-done.grad_ref, bf16[256,768]{1,0:T(8,128)(2,1)} %dynamic-slice_bitcast_fusion.2.query_ref, ...), custom_call_target="tpu_custom_call" | custom-call | flops 503316480 | bytes 2752512 | tf_op jit(solution)/shard_map/pallas_call | solution.py:42
  156.6 10.4 %collective-permute-done.3 = bf16[256,768]{1,0:T(8,128)(2,1)S(1)} collective-permute-done((bf16[256,768]{1,0:T(8,128)(2,1)S(1)}, bf16[256,768]{1,0:T(8,128)(2,1)S(1)}, u32[]{:S(2)}, u32[]{:S(2)}) %collective-permute-start.3) | collective-permute-done | bytes 393248 | tf_op jit(solution)/shard_map/ppermute | solution.py:124
  170.8 7.9 %reduce-scatter.3.cloned.1.call-done.grad_ref = bf16[256,768]{1,0:T(8,128)(2,1)} async-done(((bf16[1024,768]{1,0:T(8,128)(2,1)}), bf16[256,768]{1,0:T(8,128)(2,1)}) %reduce-scatter.3.cloned.1.call-update) | async-done | bytes 393232 | tf_op jit(solution)/shard_map/reduce_scatter | solution.py:115
  185.3 30.9 %all-gather.11.cloned.1.call-done = bf16[1024,768]{1,0:T(8,128)(2,1)} async-done(((bf16[256,768]{1,0:T(8,128)(2,1)}), bf16[1024,768]{1,0:T(8,128)(2,1)}) %all-gather.11.cloned.1.call-update) | async-done | bytes 1572880 | tf_op jit(solution)/shard_map/all_gather | solution.py:134
  221.5 41.4 %collective-permute-done.2 = bf16[256,768]{1,0:T(8,128)(2,1)S(1)} collective-permute-done((bf16[256,768]{1,0:T(8,128)(2,1)S(1)}, bf16[256,768]{1,0:T(8,128)(2,1)S(1)}, u32[]{:S(2)}, u32[]{:S(2)}) %collective-permute-start.2) | collective-permute-done | bytes 393248 | tf_op jit(solution)/shard_map/ppermute | solution.py:124
  265.0 9.5 %conditional.12 = (f32[1024,1536]{1,0:T(8,128)}) conditional(s32[]{:T(128)} %convert_element_type.28, (bf16[1024,768]{1,0:T(8,128)(2,1)S(1)}, bf16[1024,768]{1,0:T(8,128)(2,1)S(1)}, bf16[1,2,1536,1536]{3,2,1,0:T(8,128)(2,1)}) %tuple.84, () %tuple.43), branch_computations={%region_2.3_spmd, %region_3.4_spmd} | conditional | flops 4838129664 | bytes 14155784 | solution.py:152
  265.2 9.3 %fusion = f32[1024,1536]{1,0:T(8,128)} fusion(bf16[1,2,1536,1536]{3,2,1,0:T(8,128)(2,1)} %get-tuple-element.55, bf16[1024,768]{1,0:T(8,128)(2,1)S(1)} %get-tuple-element.54, bf16[1024,768]{1,0:T(8,128)(2,1)S(1)} %get-tuple-element.53), kind=kOutput, calls=%fused_computation | convolution fusion | flops 4838129664 | bytes 14155776 | tf_op jit(solution)/shard_map/cond/branch_0_fun/dot_general | solution.py:57
  280.1 9.1 %conditional.13 = (bf16[1024,1536]{1,0:T(8,128)(2,1)S(1)}) conditional(s32[]{:T(128)} %convert_element_type.28, (bf16[1,2,1536,1536]{3,2,1,0:T(8,128)(2,1)}, bf16[1024,1536]{1,0:T(8,128)(2,1)}, f32[1024,1536]{1,0:T(8,128)}) %tuple.44, (bf16[1,2,1536,1536]{3,2,1,0:T(8,128)(2,1)}, bf16[1024,1536]{1,0:T(8,128)(2,1)}) %tuple.45), branch_computations={%region_4.5_spmd, %region_5.6_spmd} | conditional | flops 4834983936 | bytes 17301512
  280.1 9.1 %fusion.10 = bf16[1024,1536]{1,0:T(8,128)(2,1)S(1)} fusion(f32[1024,1536]{1,0:T(8,128)} %get-tuple-element.58, bf16[1024,1536]{1,0:T(8,128)(2,1)} %get-tuple-element.56, bf16[1,2,1536,1536]{3,2,1,0:T(8,128)(2,1)} %get-tuple-element.57), kind=kOutput, calls=%fused_computation.10 | convolution fusion | flops 4834983936 | bytes 17301504 | tf_op jit(solution)/shard_map/cond/branch_0_fun/dot_general | solution.py:57
  289.5 39.5 %all_to_all.46 = bf16[4,256,1536]{2,1,0:T(8,128)(2,1)S(1)} all-to-all(bf16[4,256,1536]{2,1,0:T(8,128)(2,1)S(1)} %bitcast.81), channel_id=1, replica_groups=mesh['section'=2,'segment'=4,'fsdp'=4] {'segment'}, dimensions={0} | all-to-all | bytes 6291456 | tf_op jit(solution)/shard_map/all_to_all | solution.py:83
  336.0 40.6 %all-to-all-done.4 = bf16[4,64,1536]{2,1,0:T(8,128)(2,1)} async-done(((bf16[4,64,1536]{2,1,0:T(8,128)(2,1)}), bf16[4,64,1536]{2,1,0:T(8,128)(2,1)}, u32[]{:S(2)}, u32[]{:S(2)}) %all-to-all-start.4) | async-done | bytes 786464 | tf_op jit(solution)/shard_map/all_to_all | solution.py:83
  380.1 9.6 %conditional.14 = (f32[1024,1536]{1,0:T(8,128)}) conditional(s32[]{:T(128)} %convert_element_type.28, (bf16[1024,768]{1,0:T(8,128)(2,1)}, bf16[1024,768]{1,0:T(8,128)(2,1)S(1)}, bf16[1,2,1536,1536]{3,2,1,0:T(8,128)(2,1)}) %tuple.46, () %tuple.47), branch_computations={%region_7.8_spmd, %region_8.9_spmd} | conditional | flops 4838129664 | bytes 14155784 | solution.py:152
  380.1 9.6 %fusion.16 = f32[1024,1536]{1,0:T(8,128)} fusion(bf16[1,2,1536,1536]{3,2,1,0:T(8,128)(2,1)} %get-tuple-element.63, bf16[1024,768]{1,0:T(8,128)(2,1)S(1)} %get-tuple-element.62, bf16[1024,768]{1,0:T(8,128)(2,1)} %get-tuple-element.61), kind=kOutput, calls=%fused_computation.14 | convolution fusion | flops 4838129664 | bytes 14155776 | tf_op jit(solution)/shard_map/cond/branch_0_fun/dot_general | solution.py:57
  389.7 8.1 %all-gather.7.cloned.1.call-done = bf16[1024,1536]{1,0:T(8,128)(2,1)} async-done(((bf16[256,1536]{1,0:T(8,128)(2,1)}), bf16[1024,1536]{1,0:T(8,128)(2,1)}) %all-gather.7.cloned.1.call-update) | async-done | bytes 3145744 | tf_op jit(solution)/shard_map/all_gather | solution.py:135
  398.7 9.3 %conditional.15 = (bf16[1024,1536]{1,0:T(8,128)(2,1)S(1)}) conditional(s32[]{:T(128)} %convert_element_type.28, (bf16[1,2,1536,1536]{3,2,1,0:T(8,128)(2,1)}, bf16[1024,1536]{1,0:T(8,128)(2,1)}, f32[1024,1536]{1,0:T(8,128)}) %tuple.49, (bf16[1,2,1536,1536]{3,2,1,0:T(8,128)(2,1)}, bf16[1024,1536]{1,0:T(8,128)(2,1)}) %tuple.50), branch_computations={%region_9.10_spmd, %region_10.11_spmd} | conditional | flops 4834983936 | bytes 17301512
  398.7 9.1 %fusion.26 = bf16[1024,1536]{1,0:T(8,128)(2,1)S(1)} fusion(f32[1024,1536]{1,0:T(8,128)} %get-tuple-element.66, bf16[1024,1536]{1,0:T(8,128)(2,1)} %get-tuple-element.64, bf16[1,2,1536,1536]{3,2,1,0:T(8,128)(2,1)} %get-tuple-element.65), kind=kOutput, calls=%fused_computation.24 | convolution fusion | flops 4834983936 | bytes 17301504 | tf_op jit(solution)/shard_map/cond/branch_0_fun/dot_general | solution.py:57
  408.3 39.5 %all_to_all.47 = bf16[4,256,1536]{2,1,0:T(8,128)(2,1)S(1)} all-to-all(bf16[4,256,1536]{2,1,0:T(8,128)(2,1)S(1)} %bitcast.82), channel_id=1, replica_groups=mesh['section'=2,'segment'=4,'fsdp'=4] {'segment'}, dimensions={0} | all-to-all | bytes 6291456 | tf_op jit(solution)/shard_map/all_to_all | solution.py:83
  449.4 23.6 %all_to_all.48 = bf16[4,64,1536]{2,1,0:T(8,128)(2,1)S(1)} all-to-all(bf16[4,64,1536]{2,1,0:T(8,128)(2,1)} %bitcast.92), channel_id=1, replica_groups=mesh['section'=2,'segment'=4,'fsdp'=4] {'fsdp'}, dimensions={0} | all-to-all | bytes 1572864 | tf_op jit(solution)/shard_map/all_to_all | solution.py:83
  473.0 14.1 %all_to_all.49 = bf16[4,64,1536]{2,1,0:T(8,128)(2,1)S(1)} all-to-all(bf16[4,64,1536]{2,1,0:T(8,128)(2,1)S(1)} %all_to_all.48), channel_id=1, replica_groups=mesh['section'=2,'segment'=4,'fsdp'=4] {'segment'}, dimensions={0} | all-to-all | bytes 1572864 | tf_op jit(solution)/shard_map/all_to_all | solution.py:83
  (79 shorter events, 86.9 us)
Async XLA Ops:
  17.3 26.4 %all-to-all-start.1 = ((bf16[4,64,1536]{2,1,0:T(8,128)(2,1)}), bf16[4,64,1536]{2,1,0:T(8,128)(2,1)S(1)}, u32[]{:S(2)}, u32[]{:S(2)}) async-start(bf16[4,64,1536]{2,1,0:T(8,128)(2,1)} %copy.19), calls=%async_computation.1 | async-start | bytes 1572864 | tf_op jit(solution)/shard_map/all_to_all | solution.py:83
  23.7 32.5 %copy-start.3 = (bf16[1,1,64,6144]{3,2,1,0:T(8,128)(2,1)S(1)}, bf16[1,1,64,6144]{3,2,1,0:T(8,128)(2,1)}, u32[]{:S(2)}) copy-start(bf16[1,1,64,6144]{3,2,1,0:T(8,128)(2,1)} %get-tuple-element.114) | copy-start | bytes 2359300
  23.7 66.9 %all-gather.15.cloned.1.call-start = ((), (), s32[]{:S(2)}) async-start(), calls=%async_computation.17 | async-start | bytes 3932160 | tf_op jit(solution)/shard_map/all_gather | solution.py:106
  26.5 29.6 %collective-permute-start.1 = (bf16[768,768]{1,0:T(8,128)(2,1)}, bf16[768,768]{1,0:T(8,128)(2,1)}, u32[]{:S(2)}, u32[]{:S(2)}) collective-permute-start(bf16[768,768]{1,0:T(8,128)(2,1)} %get-tuple-element.97), channel_id=1, source_target_pairs={{16,0},{17,1},{18,2},{19,3},{20,4},{21,5},{22,6},{23,7},{24,8},{25... | collective-permute-start | bytes 3538952 | tf_op jit(solution)/shard_map/ppermute | solution.py:75
  43.8 12.4 %copy-start = (bf16[4,64,1536]{2,1,0:T(8,128)(2,1)}, bf16[4,64,1536]{2,1,0:T(8,128)(2,1)S(1)}, u32[]{:S(2)}) copy-start(bf16[4,64,1536]{2,1,0:T(8,128)(2,1)S(1)} %all-to-all-done.1) | copy-start | bytes 2359300
  57.8 23.4 %all-to-all-start = ((bf16[4,64,1536]{2,1,0:T(8,128)(2,1)}), bf16[4,64,1536]{2,1,0:T(8,128)(2,1)S(1)}, u32[]{:S(2)}, u32[]{:S(2)}) async-start(bf16[4,64,1536]{2,1,0:T(8,128)(2,1)} %copy.18), calls=%async_computation | async-start | bytes 1572864 | tf_op jit(solution)/shard_map/all_to_all | solution.py:83
  62.6 86.1 %reduce-scatter.5.cloned.1.call-start = ((), (), s32[]{:S(2)}) async-start(), calls=%async_computation.13 | async-start | bytes 1966080 | tf_op jit(solution)/shard_map/reduce_scatter | solution.py:115
  62.6 27.9 %collective-permute-start = (bf16[768,768]{1,0:T(8,128)(2,1)S(1)}, bf16[768,768]{1,0:T(8,128)(2,1)}, u32[]{:S(2)}, u32[]{:S(2)}) collective-permute-start(bf16[768,768]{1,0:T(8,128)(2,1)S(1)} %get-tuple-element.98), channel_id=1, source_target_pairs={{16,0},{17,1},{18,2},{19,3},{20,4},{21,5},{22,6},{23,7},{24,8},{25... | collective-permute-start | bytes 3538952 | tf_op jit(solution)/shard_map/ppermute | solution.py:76
  97.8 80.9 %reduce-scatter.3.cloned.1.call-start = ((), (), s32[]{:S(2)}) async-start(), calls=%async_computation.11 | async-start | bytes 1966080 | tf_op jit(solution)/shard_map/reduce_scatter | solution.py:115
  142.7 2.0 copy-start.4
  144.0 72.3 %all-gather.11.cloned.1.call-start = ((), (), s32[]{:S(2)}) async-start(), calls=%async_computation.15 | async-start | bytes 1966080 | tf_op jit(solution)/shard_map/all_gather | solution.py:134
  144.6 2.4 copy-start.5
  147.0 1.1 copy-start.6
  155.4 124.7 %all-gather.9.cloned.1.call-start = ((), (), s32[]{:S(2)}) async-start(), calls=%async_computation.14 | async-start | bytes 3932160 | tf_op jit(solution)/shard_map/all_gather | solution.py:135
  156.5 10.5 %collective-permute-start.3 = (bf16[256,768]{1,0:T(8,128)(2,1)S(1)}, bf16[256,768]{1,0:T(8,128)(2,1)S(1)}, u32[]{:S(2)}, u32[]{:S(2)}) collective-permute-start(bf16[256,768]{1,0:T(8,128)(2,1)S(1)} %broadcast_select_fusion.2), channel_id=1, source_target_pairs={{0,16},{16,0},{1,17},{17,1},{2,18},{18,2},{3,19},{19,3},{4,20},{20... | collective-permute-start | bytes 1179656 | tf_op jit(solution)/shard_map/ppermute | solution.py:124
  169.0 165.7 %all-gather.13.cloned.1.call-start = ((), (), s32[]{:S(2)}) async-start(), calls=%async_computation.16 | async-start | bytes 1966080 | tf_op jit(solution)/shard_map/all_gather | solution.py:134
  185.3 212.5 %all-gather.7.cloned.1.call-start = ((), (), s32[]{:S(2)}) async-start(), calls=%async_computation.12 | async-start | bytes 3932160 | tf_op jit(solution)/shard_map/all_gather | solution.py:135
  216.2 48.7 %copy-start.7 = (bf16[1024,768]{1,0:T(8,128)(2,1)S(1)}, bf16[1024,768]{1,0:T(8,128)(2,1)}, u32[]{:S(2)}) copy-start(bf16[1024,768]{1,0:T(8,128)(2,1)} %all-gather.11.cloned.1.call-done) | copy-start | bytes 4718596
  216.2 48.7 %collective-permute-start.4 = (bf16[1024,768]{1,0:T(8,128)(2,1)}, bf16[1024,768]{1,0:T(8,128)(2,1)S(1)}, u32[]{:S(2)}, u32[]{:S(2)}) collective-permute-start(bf16[1024,768]{1,0:T(8,128)(2,1)} %all-gather.11.cloned.1.call-done), channel_id=1, source_target_pairs={{16,0},{17,1},{18,2},{19,3},{20,4},{21,5},{22,6},{23,7},{24,8},{25... | collective-permute-start | bytes 4718600 | tf_op jit(solution)/shard_map/ppermute | solution.py:138
  218.7 44.2 %collective-permute-start.2 = (bf16[256,768]{1,0:T(8,128)(2,1)S(1)}, bf16[256,768]{1,0:T(8,128)(2,1)S(1)}, u32[]{:S(2)}, u32[]{:S(2)}) collective-permute-start(bf16[256,768]{1,0:T(8,128)(2,1)S(1)} %broadcast_select_fusion.5), channel_id=1, source_target_pairs={{0,16},{16,0},{1,17},{17,1},{2,18},{18,2},{3,19},{19,3},{4,20},{20... | collective-permute-start | bytes 1179656 | tf_op jit(solution)/shard_map/ppermute | solution.py:124
  330.5 46.1 %all-to-all-start.4 = ((bf16[4,64,1536]{2,1,0:T(8,128)(2,1)}), bf16[4,64,1536]{2,1,0:T(8,128)(2,1)}, u32[]{:S(2)}, u32[]{:S(2)}) async-start(bf16[4,64,1536]{2,1,0:T(8,128)(2,1)} %bitcast.91), calls=%async_computation.6 | async-start | bytes 1572864 | tf_op jit(solution)/shard_map/all_to_all | solution.py:83
  334.7 45.4 %collective-permute-start.5 = (bf16[1024,768]{1,0:T(8,128)(2,1)}, bf16[1024,768]{1,0:T(8,128)(2,1)S(1)}, u32[]{:S(2)}, u32[]{:S(2)}) collective-permute-start(bf16[1024,768]{1,0:T(8,128)(2,1)} %all-gather.13.cloned.1.call-done), channel_id=1, source_target_pairs={{16,0},{17,1},{18,2},{19,3},{20,4},{21,5},{22,6},{23,7},{24,8},{25... | collective-permute-start | bytes 4718600 | tf_op jit(solution)/shard_map/ppermute | solution.py:138
  376.6 21.2 %all-to-all-start.5 = ((bf16[4,64,1536]{2,1,0:T(8,128)(2,1)}), bf16[4,64,1536]{2,1,0:T(8,128)(2,1)S(1)}, u32[]{:S(2)}, u32[]{:S(2)}) async-start(bf16[4,64,1536]{2,1,0:T(8,128)(2,1)} %all-to-all-done.4), calls=%async_computation.7 | async-start | bytes 1572864 | tf_op jit(solution)/shard_map/all_to_all | solution.py:83
  449.4 37.7 %copy-start.2 = (bf16[4,64,1536]{2,1,0:T(8,128)(2,1)S(1)}, bf16[4,64,1536]{2,1,0:T(8,128)(2,1)}, u32[]{:S(2)}) copy-start(bf16[4,64,1536]{2,1,0:T(8,128)(2,1)} %copy-done.1) | copy-start | bytes 2359300
  (1 other events, 0.9 us)
Sparse Core Ops, SparseCore 0:
  56.3 28.7 all-gather.14
  97.9 35.5 reduce-scatter.4
  144.1 34.5 reduce-scatter.2
  180.1 36.0 all-gather.10
  217.7 62.3 all-gather.8
  281.5 35.7 all-gather.12
  318.8 78.9 all-gather.6
